TPU v7x, 128 devices: a whole 4x4x4 slice. The times are simulated.
128 devices in a mesh: freq: 4 (over z), space: 32 (over y, x, core).
Axes of the slice: x: 4, y: 4, z: 4, core: 2. Of those that a mesh axis runs over, the one named last changes fastest.
Arguments:
- segments: bfloat16 [128, 256, 32768], P('freq', None, 'space'), may hold values from -6 to 6
- volumes: float32 [32768], P('space'), may hold values from 0.03 to 3.4, as said below
- freq_bins: int32 [16], replicated, may hold values from 1 to 127, as said below
Outputs:
- modes: float32 [16, 32768, 256], P('freq', 'space')
- triangle: float32 [16, 256, 256], P('freq')
Inputs may be any that keep to these rules, and one draw needn't show every extreme that they name: `volumes`: positive weights. `freq_bins`: distinct bins; the first two are 1 and 127.
All inputs are finite; a program needn't handle non-finite values.
Results may differ from a plain program's by a relative error of at most 0.0027.
Values sent between devices are 32-bit elements; how exact they have to be, the bound alone decides.
No kernel may reach another device: no remote copies, remote signals or barrier semaphores. Data moves between devices by JAX's collectives and lax.ppermute only.
A program may use at most 128 MiB of HBM per device.

v0:
```python
from functools import partial
import math

import jax
import jax.numpy as jnp
from jax import lax
from jax.sharding import PartitionSpec as P


def make_table(freq_bins, fft_len):
    steps_t = jnp.arange(fft_len, dtype=jnp.int32)
    phase = freq_bins[:, None] * steps_t[None, :] % fft_len
    angle = 2.0 * math.pi / fft_len * phase.astype(jnp.float32)
    window = 0.5 - 0.5 * jnp.cos(2.0 * math.pi / fft_len * steps_t.astype(jnp.float32))
    scale = window / math.sqrt(fft_len)
    return jnp.stack([scale * jnp.cos(angle), -scale * jnp.sin(angle)]).astype(jnp.bfloat16)


def on_device(segments, volumes, freq_bins):
    fft_len = segments.shape[1]
    row_count = segments.shape[2]
    dft_table = make_table(freq_bins, fft_len)
    coefficients = jnp.einsum(
        "cft,btx->fxcb", dft_table, segments, preferred_element_type=jnp.float32
    )
    arrived = lax.all_to_all(coefficients, "freq", split_axis=0, concat_axis=3, tiled=True)
    freq_local, local_rows, two_parts, block_count = arrived.shape
    matrix = arrived.reshape(freq_local, local_rows, two_parts * block_count)
    weighted = matrix * volumes[None, :, None]
    gram = jnp.einsum("frc,frd->fcd", matrix, weighted, precision=lax.Precision.HIGHEST)
    gram_sum = lax.psum(gram, "space")
    lower_tri = jnp.linalg.cholesky(gram_sum)
    solve_one = partial(jax.scipy.linalg.solve_triangular, lower=True)
    basis_t = jax.vmap(solve_one)(lower_tri, jnp.swapaxes(matrix, 1, 2))
    root_rows = math.sqrt(row_count * lax.axis_size("space"))
    modes = jnp.swapaxes(basis_t, 1, 2) * root_rows
    triangle = jnp.swapaxes(lower_tri, 1, 2) / root_rows
    return (modes, triangle)


def solution(mesh):
    placed = (P("freq", None, "space"), P("space"), P())
    return jax.shard_map(
        on_device,
        mesh=mesh,
        in_specs=placed,
        out_specs=(P("freq", "space", None), P("freq", None, None)),
        check_vma=False,
    )
```

profile of v0, /device:TPU:1, one launch (start us, length us, event | category | flops | bytes accessed | tf_op | source)
XLA Modules:
  0.0 433.0 jit_solution(9234419438057238949)
XLA Ops:
  7.2 0.0 all-reduce.3.cloned.1.call-start
  7.3 0.8 multiply_convert_fusion.1
  8.1 8.8 %fusion.5 = f32[16,1024,2,32]{1,0,3,2:T(8,128)S(1)} fusion(bf16[32,256,1024]{2,1,0:T(8,128)(2,1)} %param.3, bf16[1,16,256]{2,1,0:T(8,128)(2,1)S(1)} %get-tuple-element.32, bf16[1,16,256]{2,1,0:T(8,128)(2,1)S(1)} %get-tuple-element.31), kind=kOutput, calls=%fused_computation.8 | convolution fusion | flops 536903680 | bytes 20987904 | tf_op jit(solution)/shard_map/cft,btx->fxcb/dot_general | solution.py:23
  16.9 2.4 copy.28
  19.3 53.5 %all_to_all.15 = f32[16,1024,2,32]{1,3,2,0:T(8,128)S(1)} all-to-all(f32[16,1024,2,32]{1,3,2,0:T(8,128)S(1)} %copy.28), channel_id=1, replica_groups=mesh['freq'=4,'space'=32] {'freq'}, dimensions={0} | all-to-all | bytes 8388608 | tf_op jit(solution)/shard_map/all_to_all | solution.py:26
  72.8 0.0 copy-start.2
  72.8 0.3 copy.29
  73.2 0.0 copy-start
  73.2 2.0 copy-done
  75.2 0.0 copy-done.2
  75.2 5.4 %fusion.2 = f32[4,256,256]{1,2,0:T(8,128)} fusion(f32[4,1024,256]{1,2,0:T(8,128)S(1)} %bitcast.58, f32[1024]{0:T(1024)S(1)} %copy-done.2), kind=kOutput, calls=%fused_computation.4 | convolution fusion | flops 3222274048 | bytes 5246976 | tf_op jit(solution)/shard_map/frc,frd->fcd/dot_general | solution.py:30
  80.5 0.0 all-reduce.3.cloned.1.call-update
  80.7 105.4 %all-reduce.3.cloned.1.call-done = f32[4,256,256]{1,2,0:T(8,128)} async-done(((f32[4,256,256]{1,2,0:T(8,128)}), f32[4,256,256]{1,2,0:T(8,128)}) %all-reduce.3.cloned.1.call-update) | async-done | bytes 1048592 | tf_op jit(solution)/shard_map/psum | solution.py:31
  186.0 1.6 copy.32
  187.6 1.4 fusion.12
  189.0 46.9 %custom-call.17 = f32[4,128,128]{2,1,0:T(8,128)S(1)} custom-call(f32[4,128,128]{2,1,0:T(8,128)S(1)} %cholesky.122), custom_call_target="Cholesky" | custom-call | tf_op jit(solution)/shard_map/jit(cholesky)/cholesky | solution.py:32
  235.9 39.5 %custom-call.18 = f32[4,1,128,128]{2,3,1,0:T(8,128)S(1)} custom-call(f32[4,1,128,128]{3,2,1,0:T(8,128)S(1)} %select_bitcast_fusion), custom_call_target="InvertDiagBlocksLowerTriangular" | custom-call | tf_op jit(solution)/shard_map/jit(cholesky)/cholesky | solution.py:32
  275.4 0.1 cholesky.117
  275.5 0.4 constant_dynamic-update-slice_fusion.1
  275.9 0.7 convolution_subtract_fusion
  276.6 46.9 %custom-call.19 = f32[4,128,128]{2,1,0:T(8,128)S(1)} custom-call(f32[4,128,128]{2,1,0:T(8,128)S(1)} %convolution_subtract_fusion), custom_call_target="Cholesky" | custom-call | tf_op jit(solution)/shard_map/jit(cholesky)/cholesky | solution.py:32
  323.5 0.1 select_reduce_fusion
  323.6 0.1 compare_reduce_fusion
  323.7 0.1 compare_reduce_fusion.1
  323.8 0.3 multiply_bitcast_fusion
  324.1 1.3 copy.39
  325.4 0.1 triangular_solve.62
  325.5 5.5 %while.1 = (s32[]{:T(128)}, f32[4,256,256]{2,1,0:T(8,128)S(1)}, s32[2,2]{1,0:T(2,128)S(1)}, f32[2,4,128,128]{3,2,0,1:T(8,128)}, s32[]{:T(128)}) while((s32[]{:T(128)}, f32[4,256,256]{2,1,0:T(8,128)S(1)}, s32[2,2]{1,0:T(2,128)S(1)}, f32[2,4,128,128]{3,2,0,1:T(8,128)}, s32[]{:T(128)}) %tuple.32), condition=%wide.while_cond, body=%wide.while_body.sunk | while | flops 2 | bytes 525421 | solution.py:34
  325.5 0.7 fusion.35
  326.2 2.1 bitcast_dynamic-update-slice_fusion.2
  328.3 0.7 fusion.35
  328.9 2.1 bitcast_dynamic-update-slice_fusion.2
  331.0 79.7 %custom-call.20 = f32[4,2,128,128]{2,3,1,0:T(8,128)S(1)} custom-call(f32[4,2,128,128]{3,2,1,0:T(8,128)} %bitcast.62), custom_call_target="InvertDiagBlocksLowerTriangular" | custom-call | tf_op jit(solution)/shard_map/vmap(jit(_solve_triangular))/triangular_solve | solution.py:34
  410.7 0.0 copy-start.1
  410.7 3.7 fusion.9
  414.4 1.9 fusion.14
  416.3 0.0 copy-done.1
  416.4 1.9 fusion.8
  418.3 2.5 fusion.4
  420.8 5.4 %copy.38 = f32[4,1024,256]{2,1,0:T(8,128)} copy(f32[4,1024,256]{1,2,0:T(8,128)} %fusion.4) | data formatting | bytes 8388608
  (11 shorter events, 0.2 us)
Async XLA Ops:
  7.2 178.9 %all-reduce.3.cloned.1.call-start = ((), (), s32[]{:S(2)}) async-start(), calls=%async_computation.1 | async-start | bytes 2097152 | tf_op jit(solution)/shard_map/psum | solution.py:31
  72.8 2.3 copy-start.2
  73.2 2.0 copy-start
  410.7 5.6 %copy-start.1 = (f32[4,4,1024,2,32]{2,4,0,3,1:T(8,128)S(1)}, f32[4,4,1024,2,32]{2,4,0,3,1:T(8,128)}, u32[]{:S(2)}) copy-start(f32[4,4,1024,2,32]{2,4,0,3,1:T(8,128)} %copy-done) | copy-start | bytes 12582916
Sparse Core Ops, SparseCore 0:
  80.7 105.2 all-reduce.2
where the time goes:
time: 433 us
  other arithmetic  218 us (50%)
  waiting for transfers between devices  105 us (24%)
  blocking collectives  53.5 us (12%)
  matrix products  22.7 us (5%)
  local copies, waits for them, and re-layouts  18.7 us (4%)
  between operations  14.2 us (3%)
    another operation x10, other arithmetic, on_device(): lower_tri = jnp.linalg.cholesky(gram_sum)  134 us
    psum x1, waiting for transfers between devices, on_device(): gram_sum = lax.psum(gram, 'space')  105 us
    another operation x3, other arithmetic, on_device(): basis_t = jax.vmap(solve_one)(lower_tri, jnp.swapaxes(matrix, 1, 2))  79.7 us
    all_to_all x1, blocking collectives, on_device(): lax.all_to_all(coefficients, 'freq', split_axis=0, concat_axis=3, tiled=T...  53.5 us
    dot_general x1, matrix products, on_device(): jnp.einsum('cft,btx->fxcb', dft_table, segments, preferred_element_type=j...  8.79 us
    unnamed x8, local copies, waits for them, and re-layouts  8.69 us
  transfers between devices with their start and end apart: 1, of which 1 were waited for; matrix products, arithmetic and copies ran while one was open for 0% of the time, Pallas kernels for 0%

commit v1 on v0

v1 whole, which is shorter than its diff:
```python
import functools
import math

import jax
import jax.numpy as jnp
from jax import lax
from jax.experimental import pallas as pl
from jax.experimental.pallas import tpu as pltpu
from jax.sharding import PartitionSpec as P

HIGHEST = lax.Precision.HIGHEST
HOPS = (0, 1, 3, 2)
GROUPS = ((0, 1), (2,), (3,))
PANEL = 32


def dot(a, b, dims, precision=None):
    return lax.dot_general(
        a, b, (dims, ((), ())), precision=precision, preferred_element_type=jnp.float32
    )


def dot3(a, b, dims):
    ah, bh = a.astype(jnp.bfloat16), b.astype(jnp.bfloat16)
    al = (a - ah.astype(jnp.float32)).astype(jnp.bfloat16)
    bl = (b - bh.astype(jnp.float32)).astype(jnp.bfloat16)
    return dot(ah, bh, dims) + (dot(ah, bl, dims) + dot(al, bh, dims))


def transform_kernel(bins_ref, seg_ref, *refs):
    outs, (table, landing) = refs[:-2], refs[-2:]
    group, fft_len = seg_ref.shape[0], seg_ref.shape[1]
    n_rows = table.shape[0]
    per_hop = n_rows // len(HOPS)
    n_local = per_hop // 2

    @pl.when((pl.program_id(0) == 0) & (pl.program_id(1) == 0))
    def _():
        me = lax.axis_index("freq")
        row = lax.broadcasted_iota(jnp.int32, (n_rows, fft_len), 0)
        step = lax.broadcasted_iota(jnp.int32, (n_rows, fft_len), 1)
        bins = jnp.zeros((n_rows, fft_len), jnp.int32)
        for h, hop in enumerate(HOPS):
            home = lax.rem(me + hop, len(HOPS))
            for j in range(n_local):
                which = bins_ref[home * n_local + j]
                bins = jnp.where(row // 2 == h * n_local + j, which, bins)
        phase = lax.rem(bins * step, fft_len)
        angle = 2.0 * math.pi / fft_len * phase.astype(jnp.float32)
        window = 0.5 - 0.5 * jnp.cos(2.0 * math.pi / fft_len * step.astype(jnp.float32))
        scale = window / math.sqrt(fft_len)
        wave = jnp.where(lax.rem(row, 2) == 0, jnp.cos(angle), -jnp.sin(angle))
        table[...] = (scale * wave).astype(jnp.bfloat16)

    for b in range(group):
        sums = dot(table[...], seg_ref[b], ((1,), (0,)))
        for k in range(landing.shape[0]):
            tile = slice(128 * k, 128 * k + 128)
            landing[k, pl.ds(b, n_rows, stride=group), :] = sums[:, tile]
    n = 0
    for js in GROUPS:
        for h in range(len(HOPS)):
            out = outs[n]
            n += 1
            for i, j in enumerate(js):
                for c in range(2):
                    r = (h * per_hop + j * 2 + c) * group
                    for k in range(landing.shape[0]):
                        tile = slice(128 * k, 128 * k + 128)
                        out[i, c, :, tile] = landing[k, r : r + group, :]


def transform(bins, segments):
    n_seg, fft_len, n_x = segments.shape
    group, cols = 8, n_x // 2
    n_rows = 2 * bins.shape[0]
    shapes, specs = [], []
    for js in GROUPS:
        for _ in HOPS:
            shapes.append(jax.ShapeDtypeStruct((len(js), 2, n_seg, n_x), jnp.float32))
            specs.append(
                pl.BlockSpec((len(js), 2, group, cols), lambda g, x: (0, 0, g, x))
            )
    outs = pl.pallas_call(
        transform_kernel,
        out_shape=shapes,
        grid=(n_seg // group, n_x // cols),
        in_specs=[
            pl.BlockSpec(memory_space=pltpu.SMEM),
            pl.BlockSpec((group, fft_len, cols), lambda g, x: (g, 0, x)),
        ],
        out_specs=specs,
        scratch_shapes=[
            pltpu.VMEM((n_rows, fft_len), jnp.bfloat16),
            pltpu.VMEM((cols // 128, n_rows * group, 128), jnp.float32),
        ],
        compiler_params=pltpu.CompilerParams(vmem_limit_bytes=40 << 20),
        cost_estimate=pl.CostEstimate(
            flops=2 * n_seg * fft_len * n_x * n_rows,
            bytes_accessed=20 << 20,
            transcendentals=0,
        ),
    )(bins, segments)
    k = len(HOPS)
    return [outs[i * k : (i + 1) * k] for i in range(len(GROUPS))]


def gram_kernel(halves, vol_ref, *refs):
    pieces, (mt_ref, mine_ref, other_ref, total) = refs[:4], refs[4:]
    me, core = lax.axis_index("freq"), lax.rem(lax.axis_index("space"), 2)
    n_seg = pieces[0].shape[2]
    n_all = n_seg * len(HOPS)
    for h, hop in enumerate(HOPS):
        source = lax.rem(me + len(HOPS) - hop, len(HOPS))
        for c in range(2):
            start = pl.multiple_of(c * n_all + source * n_seg, n_seg)
            mt_ref[0, pl.ds(start, n_seg), :] = pieces[h][0, c]
    m = mt_ref[0]
    g = dot3(m, m * vol_ref[...], ((1,), (1,)))
    n = m.shape[0] // 2
    blocks = (g[:n, :n], g[n:, :n], g[n:, n:])
    if halves:
        for i, block in enumerate(blocks):
            total[i] = block
        k = n // 2
        mine_ref[...] = total[:, pl.ds(pl.multiple_of(core * k, k), k), :]
        other_ref[...] = total[:, pl.ds(pl.multiple_of((1 - core) * k, k), k), :]
    else:

        @pl.when(pl.program_id(0) == core)
        def _():
            for i, block in enumerate(blocks):
                mine_ref[i] = block

        @pl.when(pl.program_id(0) != core)
        def _():
            for i, block in enumerate(blocks):
                other_ref[i] = block


def gram(volumes, pieces):
    nj, two, n_seg, n_x = pieces[0].shape
    n = two * n_seg * len(HOPS)
    halves = nj == 1
    part = (3, n // 4 if halves else n // 2, n // 2)
    piece = pl.BlockSpec((1, two, n_seg, n_x), lambda j: (j, 0, 0, 0))
    whole = pl.BlockSpec(part, lambda j: (0, 0, 0))
    return pl.pallas_call(
        functools.partial(gram_kernel, halves),
        out_shape=[
            jax.ShapeDtypeStruct((nj, n, n_x), jnp.float32),
            jax.ShapeDtypeStruct(part, jnp.float32),
            jax.ShapeDtypeStruct(part, jnp.float32),
        ],
        grid=(nj,),
        in_specs=[pl.BlockSpec((1, n_x), lambda j: (0, 0))] + [piece] * len(HOPS),
        out_specs=[pl.BlockSpec((1, n, n_x), lambda j: (j, 0, 0)), whole, whole],
        scratch_shapes=[pltpu.VMEM((3, n // 2, n // 2), jnp.float32)],
        compiler_params=pltpu.CompilerParams(vmem_limit_bytes=40 << 20),
        cost_estimate=pl.CostEstimate(
            flops=6 * nj * n * n * n_x,
            bytes_accessed=8 * nj * n * n_x,
            transcendentals=0,
        ),
    )(volumes.reshape(1, n_x), *pieces)


def space_pairs(kind):
    pairs = []
    for i in range(32):
        y, x, core = i // 8, i // 2 % 4, i % 2
        if kind == "core":
            core = 1 - core
        else:
            along_x = (kind < 2) == (core == 0)
            flip = (lambda v: v ^ 1) if kind % 2 == 0 else (lambda v: 3 - v)
            x, y = (flip(x), y) if along_x else (x, flip(y))
        pairs.append((i, (y * 4 + x) * 2 + core))
    return pairs


def swap(value, kind):
    return lax.ppermute(value, "space", space_pairs(kind))


def sum_over_space(mine, other):
    value = mine + swap(other, "core")
    for kind in range(4):
        value = value + swap(value, kind)
    return value


def factor(work):
    n = work.shape[0]
    rows = lax.broadcasted_iota(jnp.int32, (8, 128), 0)
    n_sub, half = PANEL // 8, n // 128
    for base in range(0, n, PANEL):
        tile, lane = base // 128, base % 128
        tiles = [
            t for t in range(2 * half)
            if (tile <= t < half) or (t >= half and (t - half) * 128 < base + PANEL)
        ]
        live = [
            {t: work[base + 8 * i : base + 8 * i + 8, 128 * t : 128 * t + 128] for t in tiles}
            for i in range(n_sub)
        ]
        done = [{} for _ in range(n_sub)]
        column = [
            {
                j: jnp.broadcast_to(live[i][tile][:, lane + j : lane + j + 1], (8, 128))
                for j in range(8 * i + 8)
            }
            for i in range(n_sub)
        ]
        for p in range(PANEL):
            ip, sp = p // 8, p % 8
            pivot = jnp.broadcast_to(column[ip][p][sp : sp + 1, :], (8, 128))
            root = lax.rsqrt(pivot)
            inv = root * root
            mult = {i: column[i][p] * inv for i in range(ip, n_sub)}
            for j in range(p + 1, PANEL):
                ij = j // 8
                entry = jnp.broadcast_to(column[ij][p][j % 8 : j % 8 + 1, :], (8, 128))
                for i in range(ij, n_sub):
                    column[i][j] = column[i][j] - mult[i] * entry
            for t in tiles:
                row = jnp.broadcast_to(live[ip][t][sp : sp + 1, :], (8, 128))
                scaled = row * root
                done[ip][t] = scaled if sp == 0 else jnp.where(rows == sp, scaled, done[ip][t])
                for i in range(ip, n_sub):
                    if i > ip or sp < 7:
                        live[i][t] = live[i][t] - mult[i] * row
        for i in range(n_sub):
            for t in tiles:
                work[base + 8 * i : base + 8 * i + 8, 128 * t : 128 * t + 128] = done[i][t]
        after = base + PANEL
        first = after // 128
        for blk in range(first, half):
            lo, hi = max(after, 128 * blk), 128 * blk + 128
            left = work[base:after, 128 * blk : hi]
            for c0, c1 in ((128 * first, n), (n, n + (after + 127) // 128 * 128)):
                right = work[base:after, c0:c1]
                update = dot(left, right, ((0,), (0,)), HIGHEST)
                work[lo:hi, c0:c1] = work[lo:hi, c0:c1] - update[lo - 128 * blk :, :]


def load_gram(work, g11, g21, g22):
    n = work.shape[0]
    h = n // 2
    work[:h, :h] = g11
    work[:h, h:n] = g21.T
    work[h:, h:n] = g22
    work[h:, :h] = g21
    r = lax.broadcasted_iota(jnp.int32, (n, n), 0)
    c = lax.broadcasted_iota(jnp.int32, (n, n), 1)
    work[:, n:] = jnp.where(r == c, 1.0, 0.0)


def masked_factors(work):
    n = work.shape[0]
    r = lax.broadcasted_iota(jnp.int32, (n, n), 0)
    c = lax.broadcasted_iota(jnp.int32, (n, n), 1)
    upper = jnp.where(r <= c, work[:, :n], 0.0)
    inverse = jnp.where(r >= c, work[:, n:], 0.0)
    return upper, inverse


def factor_kernel(g_ref, out_ref, work):
    load_gram(work, g_ref[0], g_ref[1], g_ref[2])
    factor(work)
    upper, inverse = masked_factors(work)
    out_ref[0] = upper
    out_ref[1] = inverse


def factor_call(blocks):
    n = 2 * blocks.shape[2]
    return pl.pallas_call(
        factor_kernel,
        out_shape=jax.ShapeDtypeStruct((2, n, n), jnp.float32),
        scratch_shapes=[pltpu.VMEM((n, 2 * n), jnp.float32)],
        compiler_params=pltpu.CompilerParams(vmem_limit_bytes=40 << 20),
        cost_estimate=pl.CostEstimate(
            flops=16 * n * n * n, bytes_accessed=12 * n * n, transcendentals=0
        ),
    )(blocks)


def modes_pair_kernel(root_rows, mine_ref, other_ref, mt_ref, *refs):
    modes_ref, tri_ref = refs[-2:]
    core = lax.rem(lax.axis_index("space"), 2)
    is_mine = pl.program_id(0) == core

    def emit(src):
        modes_ref[0] = dot(mt_ref[0], src[1] * root_rows, ((0,), (1,)), HIGHEST)
        tri_ref[0] = src[0] * (1.0 / root_rows)

    @pl.when(is_mine)
    def _():
        emit(mine_ref)

    @pl.when(jnp.logical_not(is_mine))
    def _():
        emit(other_ref)


def modes_one_kernel(root_rows, mine_ref, other_ref, mt_ref, *refs):
    modes_ref, tri_ref, work, g = refs[-4:]

    @pl.when(pl.program_id(0) == 0)
    def _():
        core = lax.rem(lax.axis_index("space"), 2)
        k = mine_ref.shape[1]
        g[:, pl.ds(pl.multiple_of(core * k, k), k), :] = mine_ref[...]
        g[:, pl.ds(pl.multiple_of((1 - core) * k, k), k), :] = other_ref[...]
        load_gram(work, g[0], g[1], g[2])
        factor(work)
        upper, inverse = masked_factors(work)
        n = work.shape[0]
        tri_ref[0] = upper * (1.0 / root_rows)
        work[:, n:] = inverse * root_rows

    n = work.shape[0]
    modes_ref[0] = dot(mt_ref[0], work[:, n:], ((0,), (1,)), HIGHEST)


def modes_call(js, n_local, root_rows, mine, other, mt, before):
    nj, n, n_x = mt.shape
    shapes = [
        jax.ShapeDtypeStruct((n_local, n_x, n), jnp.float32),
        jax.ShapeDtypeStruct((n_local, n, n), jnp.float32),
    ]
    whole = pl.BlockSpec(mine.shape, lambda j: (0,) * mine.ndim)
    first = js[0]
    if nj == 1:
        parts = 4
        body, scratch = modes_one_kernel, [
            pltpu.VMEM((n, 2 * n), jnp.float32),
            pltpu.VMEM((3, n // 2, n // 2), jnp.float32),
        ]
        grid = (parts,)
        mt_spec = pl.BlockSpec((1, n, n_x // parts), lambda x: (0, 0, x))
        out_specs = [
            pl.BlockSpec((1, n_x // parts, n), lambda x: (first, x, 0)),
            pl.BlockSpec((1, n, n), lambda x: (first, 0, 0)),
        ]
    else:
        body, scratch = modes_pair_kernel, []
        grid = (nj,)
        mt_spec = pl.BlockSpec((1, n, n_x), lambda j: (j, 0, 0))
        out_specs = [
            pl.BlockSpec((1, n_x, n), lambda j: (first + j, 0, 0)),
            pl.BlockSpec((1, n, n), lambda j: (first + j, 0, 0)),
        ]
    before = list(before)
    return pl.pallas_call(
        functools.partial(body, root_rows),
        out_shape=shapes,
        grid=grid,
        in_specs=[whole, whole, mt_spec] + [pl.BlockSpec(memory_space=pl.ANY)] * len(before),
        out_specs=out_specs,
        scratch_shapes=scratch,
        input_output_aliases={3 + i: i for i in range(len(before))},
        compiler_params=pltpu.CompilerParams(vmem_limit_bytes=40 << 20),
        cost_estimate=pl.CostEstimate(
            flops=12 * nj * n * n * n_x,
            bytes_accessed=8 * nj * n * n_x,
            transcendentals=0,
        ),
    )(mine, other, mt, *before)


def on_device(segments, volumes, freq_bins):
    n_freq = lax.axis_size("freq")
    n_local = freq_bins.shape[0] // n_freq
    root_rows = math.sqrt(segments.shape[2] * lax.axis_size("space"))
    sent = transform(freq_bins, segments)
    outs = ()
    previous = None
    arrived = []
    for js, pieces in zip(GROUPS, sent):
        got = [pieces[0]]
        for h, hop in enumerate(HOPS):
            if hop == 0:
                continue
            piece = pieces[h]
            if previous is not None:
                piece, previous[h] = lax.optimization_barrier((piece, previous[h]))
            got.append(lax.ppermute(piece, "freq", [(i, (i + hop) % n_freq) for i in range(n_freq)]))
        if previous is not None:
            arrived[-1] = previous
        previous = list(got)
        arrived.append(previous)
    grams = [gram(volumes, got) for got in arrived]
    for js, (mt, mine, other) in zip(GROUPS, grams):
        value = sum_over_space(mine, other)
        if len(js) == 2:
            value = factor_call(value)
        outs = modes_call(js, n_local, root_rows, value, swap(value, "core"), mt, outs)
    return tuple(outs)


def solution(mesh):
    placed = (P("freq", None, "space"), P("space"), P())
    return jax.shard_map(
        on_device,
        mesh=mesh,
        in_specs=placed,
        out_specs=(P("freq", "space", None), P("freq", None, None)),
        check_vma=False,
    )
```

time: 433 us -> 136 us (0.31)
  other arithmetic: 218 us -> 0.26 us
  waiting for transfers between devices: 105 us -> 48.4 us
  blocking collectives: 53.5 us -> 0 us
  Pallas kernels: 0 us -> 45 us
  starting transfers between devices: 0.04 us -> 40.7 us
  matrix products: 22.7 us -> 0 us
  local copies, waits for them, and re-layouts: 18.7 us -> 0.65 us
  between operations: 14.2 us -> 0.75 us
    another operation x14 -> x0, other arithmetic: 214 us -> none  [the longest x10 134 us: on_device(): lower_tri = jnp.linalg.cholesky(gram_sum)]
    psum x1 -> x0, waiting for transfers between devices: 105 us -> none  [on_device(): gram_sum = lax.psum(gram, 'space')]
    all_to_all x1 -> x0, blocking collectives: 53.5 us -> none  [on_device(): lax.all_to_all(coefficients, 'freq', split_axis=0, concat_axis=3, tiled=T...]
    ppermute x0 -> x27, waiting for transfers between devices: none -> 48.4 us  [the longest x9 31.9 us: on_device(): lax.ppermute(piece, 'freq', [(i, (i + hop) % n_freq) for i in range(n_fre...]
    pallas_call x0 -> x8, Pallas kernels: none -> 45 us  [the longest x3 24 us: modes_call(): pl.pallas_call(functools.partial(body, root_rows), out_shape=shapes, grid...]
    ppermute x0 -> x27, starting transfers between devices: none -> 40.7 us  [the longest x18 26.9 us: swap(): return lax.ppermute(value, 'space', space_pairs(kind))]
    dot_general x2 -> x0, matrix products: 14.1 us -> none  [the longest x1 8.79 us: on_device(): jnp.einsum('cft,btx->fxcb', dft_table, segments, preferred_element_type=j...]
    another operation x5 -> x0, matrix products: 8.58 us -> none  [the longest x3 7.53 us: on_device(): basis_t = jax.vmap(solve_one)(lower_tri, jnp.swapaxes(matrix, 1, 2))]
  transfers between devices with their start and end apart: 1 -> 27, of which waited for: 1 -> 15; matrix products, arithmetic and copies ran while one was open for 0% -> 0% of each run, Pallas kernels for 0% -> 17%
where the time goes in v1:
time: 136 us
  waiting for transfers between devices  48.4 us (36%)
  Pallas kernels  45 us (33%)
  starting transfers between devices  40.7 us (30%)
    ppermute x9, waiting for transfers between devices, on_device(): lax.ppermute(piece, 'freq', [(i, (i + hop) % n_freq) for i in range(n_fre...  31.9 us
    ppermute x18, starting transfers between devices, swap(): return lax.ppermute(value, 'space', space_pairs(kind))  26.9 us
    pallas_call x3, Pallas kernels, modes_call(): pl.pallas_call(functools.partial(body, root_rows), out_shape=shapes, grid...  24 us
    ppermute x18, waiting for transfers between devices, swap(): return lax.ppermute(value, 'space', space_pairs(kind))  16.4 us
    ppermute x9, starting transfers between devices, on_device(): lax.ppermute(piece, 'freq', [(i, (i + hop) % n_freq) for i in range(n_fre...  13.9 us
    pallas_call x1, Pallas kernels, transform(): pl.pallas_call(transform_kernel, out_shape=shapes, grid=(n_seg // group,...  10.3 us
    pallas_call x1, Pallas kernels, factor_call(): pl.pallas_call(factor_kernel, out_shape=jax.ShapeDtypeStruct((2, n, n), j...  7.7 us
    pallas_call x3, Pallas kernels, gram(): pl.pallas_call(functools.partial(gram_kernel, halves), out_shape=[jax.Sha...  3.08 us
  transfers between devices with their start and end apart: 27, of which 15 were waited for; matrix products, arithmetic and copies ran while one was open for 0% of the time, Pallas kernels for 17%

profile of v1, /device:TPU:1, one launch (start us, length us, event | category | flops | bytes accessed | tf_op | source)
XLA Modules:
  0.0 135.8 jit_solution(3003903974613216616)
XLA Ops:
  0.6 0.0 copy-start
  0.6 0.6 copy-done
  1.3 10.3 %shard_map.50 = (f32[2,2,32,1024]{3,2,1,0:T(8,128)S(1)}, f32[2,2,32,1024]{3,2,1,0:T(8,128)S(1)}, f32[2,2,32,1024]{3,2,1,0:T(8,128)S(1)}, f32[2,2,32,1024]{3,2,1,...) custom-call(s32[16]{0:T(128)S(1)} %copy-done, ...), custom_call_target="tpu_custom_call" | custom-call | flops 536870912 | bytes 20971520 | tf_op jit(solution)/shard_map/pallas_call | solution.py:84
  11.6 4.5 %collective-permute-start.6 = (f32[2,2,32,1024]{3,2,1,0:T(8,128)S(1)}, f32[2,2,32,1024]{3,2,1,0:T(8,128)S(1)}, u32[]{:S(2)}, u32[]{:S(2)}) collective-permute-start(f32[2,2,32,1024]{3,2,1,0:T(8,128)S(1)} %get-tuple-element.52), channel_id=1, source_target_pairs={{0,64},{32,96},{64,0},{96,32},{1,65},{33,97},{65,1},{97,33},{2,66}... | collective-permute-start | bytes 1572872 | tf_op jit(solution)/shard_map/ppermute | solution.py:389
  16.1 0.4 collective-permute-start.3
  16.5 1.0 collective-permute-start
  17.5 10.2 %collective-permute-done.6.refs_3_ = f32[2,2,32,1024]{3,2,1,0:T(8,128)S(1)} collective-permute-done((f32[2,2,32,1024]{3,2,1,0:T(8,128)S(1)}, f32[2,2,32,1024]{3,2,1,0:T(8,128)S(1)}, u32[]{:S(2)}, u32[]{:S(2)}) %collective-permute-start.6) | collective-permute-done | bytes 524320 | tf_op jit(solution)/shard_map/ppermute | solution.py:389
  27.8 11.7 %collective-permute-done.3.refs_2_ = f32[2,2,32,1024]{3,2,1,0:T(8,128)S(1)} collective-permute-done((f32[2,2,32,1024]{3,2,1,0:T(8,128)S(1)}, f32[2,2,32,1024]{3,2,1,0:T(8,128)S(1)}, u32[]{:S(2)}, u32[]{:S(2)}) %collective-permute-start.3) | collective-permute-done | bytes 524320 | tf_op jit(solution)/shard_map/ppermute | solution.py:389
  39.5 0.2 collective-permute-done.refs_1_
  39.7 1.5 %shard_map.53 = (f32[2,256,1024]{2,1,0:T(8,128)S(1)}, f32[3,128,128]{2,1,0:T(8,128)S(1)}, f32[3,128,128]{2,1,0:T(8,128)S(1)}) custom-call(f32[1,1024]{1,0:T(1,128)S(1)} %bitcast.1, f32[2,2,32,1024]{3,2,1,0:T(8,128)S(1)} %get-tuple-element.65.refs_0_, f32[2,2,32,1024]{3,2,1,0:T(8,128)S(1)} %collective-permute-done.refs_1_, ...), custom_call_target="tpu_custom_call" | custom-call | flops 805306368 | bytes 4194304 | tf_op jit(solution)/shard_map/pallas_call | solution.py:148
  41.2 1.3 collective-permute-start.21
  42.5 1.1 collective-permute-done.21
  43.6 1.4 %collective-permute-start.22 = (f32[3,128,128]{2,1,0:T(8,128)S(1)}, f32[3,128,128]{2,1,0:T(8,128)S(1)}, u32[]{:S(2)}, u32[]{:S(2)}) collective-permute-start(f32[3,128,128]{2,1,0:T(8,128)S(1)} %add.55), channel_id=1, source_target_pairs={{0,2},{1,9},{2,0},{3,11},{4,6},{5,13},{6,4},{7,15},{8,10},{9,1},{1... | collective-permute-start | bytes 589832 | tf_op jit(solution)/shard_map/ppermute | solution.py:183
  45.0 3.5 %collective-permute-done.22 = f32[3,128,128]{2,1,0:T(8,128)S(1)} collective-permute-done((f32[3,128,128]{2,1,0:T(8,128)S(1)}, f32[3,128,128]{2,1,0:T(8,128)S(1)}, u32[]{:S(2)}, u32[]{:S(2)}) %collective-permute-start.22) | collective-permute-done | bytes 196640 | tf_op jit(solution)/shard_map/ppermute | solution.py:183
  48.6 2.8 %collective-permute-start.23 = (f32[3,128,128]{2,1,0:T(8,128)S(1)}, f32[3,128,128]{2,1,0:T(8,128)S(1)}, u32[]{:S(2)}, u32[]{:S(2)}) collective-permute-start(f32[3,128,128]{2,1,0:T(8,128)S(1)} %add.56), channel_id=1, source_target_pairs={{0,6},{1,25},{2,4},{3,27},{4,2},{5,29},{6,0},{7,31},{8,14},{9,17},... | collective-permute-start | bytes 589832 | tf_op jit(solution)/shard_map/ppermute | solution.py:183
  51.4 2.2 %collective-permute-start.7 = (f32[1,2,32,1024]{3,2,1,0:T(8,128)S(1)}, f32[1,2,32,1024]{3,2,1,0:T(8,128)S(1)}, u32[]{:S(2)}, u32[]{:S(2)}) collective-permute-start(f32[1,2,32,1024]{3,2,1,0:T(8,128)S(1)} %get-tuple-element.53), channel_id=1, source_target_pairs={{0,64},{32,96},{64,0},{96,32},{1,65},{33,97},{65,1},{97,33},{2,66}... | collective-permute-start | bytes 786440 | tf_op jit(solution)/shard_map/ppermute | solution.py:389
  53.6 0.9 collective-permute-start.4
  54.5 0.5 collective-permute-start.1
  55.0 0.0 collective-permute-done.23
  55.1 1.3 collective-permute-start.24
  56.4 3.1 %collective-permute-done.7.refs_3_ = f32[1,2,32,1024]{3,2,1,0:T(8,128)S(1)} collective-permute-done((f32[1,2,32,1024]{3,2,1,0:T(8,128)S(1)}, f32[1,2,32,1024]{3,2,1,0:T(8,128)S(1)}, u32[]{:S(2)}, u32[]{:S(2)}) %collective-permute-start.7) | collective-permute-done | bytes 262176 | tf_op jit(solution)/shard_map/ppermute | solution.py:389
  59.4 6.2 %collective-permute-done.4.refs_2_ = f32[1,2,32,1024]{3,2,1,0:T(8,128)S(1)} collective-permute-done((f32[1,2,32,1024]{3,2,1,0:T(8,128)S(1)}, f32[1,2,32,1024]{3,2,1,0:T(8,128)S(1)}, u32[]{:S(2)}, u32[]{:S(2)}) %collective-permute-start.4) | collective-permute-done | bytes 262176 | tf_op jit(solution)/shard_map/ppermute | solution.py:389
  65.6 0.5 collective-permute-done.1.refs_1_
  66.1 2.8 %collective-permute-start.8 = (f32[1,2,32,1024]{3,2,1,0:T(8,128)S(1)}, f32[1,2,32,1024]{3,2,1,0:T(8,128)S(1)}, u32[]{:S(2)}, u32[]{:S(2)}) collective-permute-start(f32[1,2,32,1024]{3,2,1,0:T(8,128)S(1)} %get-tuple-element.54), channel_id=1, source_target_pairs={{0,64},{32,96},{64,0},{96,32},{1,65},{33,97},{65,1},{97,33},{2,66}... | collective-permute-start | bytes 786440 | tf_op jit(solution)/shard_map/ppermute | solution.py:389
  68.9 0.9 collective-permute-start.5
  69.8 0.5 collective-permute-start.2
  70.4 0.0 collective-permute-done.24
  70.4 2.1 %collective-permute-start.25 = (f32[3,128,128]{2,1,0:T(8,128)S(1)}, f32[3,128,128]{2,1,0:T(8,128)S(1)}, u32[]{:S(2)}, u32[]{:S(2)}) collective-permute-start(f32[3,128,128]{2,1,0:T(8,128)S(1)} %add.58), channel_id=1, source_target_pairs={{0,24},{1,7},{2,26},{3,5},{4,28},{5,3},{6,30},{7,1},{8,16},{9,15},... | collective-permute-start | bytes 589832 | tf_op jit(solution)/shard_map/ppermute | solution.py:183
  72.5 0.8 shard_map.52
  73.3 0.3 collective-permute-start.15
  73.6 3.0 %collective-permute-done.25 = f32[3,128,128]{2,1,0:T(8,128)S(1)} collective-permute-done((f32[3,128,128]{2,1,0:T(8,128)S(1)}, f32[3,128,128]{2,1,0:T(8,128)S(1)}, u32[]{:S(2)}, u32[]{:S(2)}) %collective-permute-start.25) | collective-permute-done | bytes 196640 | tf_op jit(solution)/shard_map/ppermute | solution.py:183
  76.6 7.7 %shard_map.54.mine_ref = f32[2,256,256]{2,1,0:T(8,128)S(1)} custom-call(f32[3,128,128]{2,1,0:T(8,128)S(1)} %add.59.g_ref), custom_call_target="tpu_custom_call" | custom-call | flops 268435456 | bytes 786432 | tf_op jit(solution)/shard_map/pallas_call | solution.py:278
  84.3 2.3 %collective-permute-start.26 = (f32[2,256,256]{2,1,0:T(8,128)S(1)}, f32[2,256,256]{2,1,0:T(8,128)S(1)}, u32[]{:S(2)}, u32[]{:S(2)}) collective-permute-start(f32[2,256,256]{2,1,0:T(8,128)S(1)} %shard_map.54.mine_ref), channel_id=1, source_target_pairs={{0,1},{1,0},{2,3},{3,2},{4,5},{5,4},{6,7},{7,6},{8,9},{9,8},{10,11... | collective-permute-start | bytes 1572872 | tf_op jit(solution)/shard_map/ppermute | solution.py:183
  86.5 0.0 collective-permute-done.8.refs_3_
  86.5 0.0 collective-permute-done.5.refs_2_
  86.5 0.0 collective-permute-done.2.refs_1_
  86.5 0.8 shard_map.51
  87.3 0.1 collective-permute-start.9
  87.5 0.0 collective-permute-done.15
  87.5 0.1 collective-permute-start.16
  87.6 1.2 collective-permute-done.9
  88.7 0.4 collective-permute-start.10
  89.1 2.2 %collective-permute-done.16 = f32[3,64,128]{2,1,0:T(8,128)S(1)} collective-permute-done((f32[3,64,128]{2,1,0:T(8,128)S(1)}, f32[3,64,128]{2,1,0:T(8,128)S(1)}, u32[]{:S(2)}, u32[]{:S(2)}) %collective-permute-start.16) | collective-permute-done | bytes 98336 | tf_op jit(solution)/shard_map/ppermute | solution.py:183
  91.3 0.2 collective-permute-start.17
  91.5 0.8 collective-permute-done.10
  92.3 1.9 %collective-permute-start.11 = (f32[3,64,128]{2,1,0:T(8,128)S(1)}, f32[3,64,128]{2,1,0:T(8,128)S(1)}, u32[]{:S(2)}, u32[]{:S(2)}) collective-permute-start(f32[3,64,128]{2,1,0:T(8,128)S(1)} %add.46), channel_id=1, source_target_pairs={{0,6},{1,25},{2,4},{3,27},{4,2},{5,29},{6,0},{7,31},{8,14},{9,17},... | collective-permute-start | bytes 294920 | tf_op jit(solution)/shard_map/ppermute | solution.py:183
  94.2 1.9 %collective-permute-done.17 = f32[3,64,128]{2,1,0:T(8,128)S(1)} collective-permute-done((f32[3,64,128]{2,1,0:T(8,128)S(1)}, f32[3,64,128]{2,1,0:T(8,128)S(1)}, u32[]{:S(2)}, u32[]{:S(2)}) %collective-permute-start.17) | collective-permute-done | bytes 98336 | tf_op jit(solution)/shard_map/ppermute | solution.py:183
  96.1 1.3 collective-permute-start.18
  97.4 0.0 collective-permute-done.11
  97.5 1.2 collective-permute-start.12
  98.7 1.3 collective-permute-done.18
  100.0 1.7 %collective-permute-start.19 = (f32[3,64,128]{2,1,0:T(8,128)S(1)}, f32[3,64,128]{2,1,0:T(8,128)S(1)}, u32[]{:S(2)}, u32[]{:S(2)}) collective-permute-start(f32[3,64,128]{2,1,0:T(8,128)S(1)} %add.53), channel_id=1, source_target_pairs={{0,24},{1,7},{2,26},{3,5},{4,28},{5,3},{6,30},{7,1},{8,16},{9,15},... | collective-permute-start | bytes 294920 | tf_op jit(solution)/shard_map/ppermute | solution.py:183
  101.6 0.0 collective-permute-done.12
  101.7 1.5 %collective-permute-start.13 = (f32[3,64,128]{2,1,0:T(8,128)S(1)}, f32[3,64,128]{2,1,0:T(8,128)S(1)}, u32[]{:S(2)}, u32[]{:S(2)}) collective-permute-start(f32[3,64,128]{2,1,0:T(8,128)S(1)} %add.48), channel_id=1, source_target_pairs={{0,24},{1,7},{2,26},{3,5},{4,28},{5,3},{6,30},{7,1},{8,16},{9,15},... | collective-permute-start | bytes 294920 | tf_op jit(solution)/shard_map/ppermute | solution.py:183
  103.2 1.5 %collective-permute-done.19 = f32[3,64,128]{2,1,0:T(8,128)S(1)} collective-permute-done((f32[3,64,128]{2,1,0:T(8,128)S(1)}, f32[3,64,128]{2,1,0:T(8,128)S(1)}, u32[]{:S(2)}, u32[]{:S(2)}) %collective-permute-start.19) | collective-permute-done | bytes 98336 | tf_op jit(solution)/shard_map/ppermute | solution.py:183
  104.7 4.6 %collective-permute-start.20 = (f32[3,64,128]{2,1,0:T(8,128)S(1)}, f32[3,64,128]{2,1,0:T(8,128)S(1)}, u32[]{:S(2)}, u32[]{:S(2)}) collective-permute-start(f32[3,64,128]{2,1,0:T(8,128)S(1)} %add.54.mine_ref), channel_id=1, source_target_pairs={{0,1},{1,0},{2,3},{3,2},{4,5},{5,4},{6,7},{7,6},{8,9},{9,8},{10,11... | collective-permute-start | bytes 294920 | tf_op jit(solution)/shard_map/ppermute | solution.py:183
  109.3 0.0 collective-permute-done.13
  109.3 2.5 %collective-permute-start.14 = (f32[3,64,128]{2,1,0:T(8,128)S(1)}, f32[3,64,128]{2,1,0:T(8,128)S(1)}, u32[]{:S(2)}, u32[]{:S(2)}) collective-permute-start(f32[3,64,128]{2,1,0:T(8,128)S(1)} %add.49.mine_ref), channel_id=1, source_target_pairs={{0,1},{1,0},{2,3},{3,2},{4,5},{5,4},{6,7},{7,6},{8,9},{9,8},{10,11... | collective-permute-start | bytes 294920 | tf_op jit(solution)/shard_map/ppermute | solution.py:183
  111.8 0.0 collective-permute-done.26.other_ref
  111.8 3.1 %shard_map.55 = (f32[4,1024,256]{2,1,0:T(8,128)}, f32[4,256,256]{2,1,0:T(8,128)}) custom-call(f32[2,256,256]{2,1,0:T(8,128)S(1)} %shard_map.54.mine_ref, f32[2,256,256]{2,1,0:T(8,128)S(1)} %collective-permute-done.26.other_ref, f32[2,256,1024]{2,1,0:T(8,128)S(1)} %get-tuple-element.71.mt_ref), custom_call_target="tpu_custom_call" | custom-call | flops 1610612736 | bytes 4194304 | tf_op jit(solution)/shard_map/pallas_call | solution.py:356
  114.9 0.0 collective-permute-done.20.other_ref
  114.9 10.4 %shard_map.56 = (f32[4,1024,256]{2,1,0:T(8,128)}, f32[4,256,256]{2,1,0:T(8,128)}) custom-call(f32[3,64,128]{2,1,0:T(8,128)S(1)} %add.54.mine_ref, f32[3,64,128]{2,1,0:T(8,128)S(1)} %collective-permute-done.20.other_ref, f32[1,256,1024]{2,1,0:T(8,128)S(1)} %get-tuple-element.64.mt_ref, ...), custom_call_target="tpu_custom_call", output_to_operand_aliasing={{0}: (3, {}), {1}: (4, {})} | custom-call | flops 805306368 | bytes 2097152 | tf_op jit(solution)/shard_map/pallas_call | solution.py:356
  125.3 0.0 collective-permute-done.14.other_ref
  125.4 10.4 %shard_map.57 = (f32[4,1024,256]{2,1,0:T(8,128)}, f32[4,256,256]{2,1,0:T(8,128)}) custom-call(f32[3,64,128]{2,1,0:T(8,128)S(1)} %add.49.mine_ref, f32[3,64,128]{2,1,0:T(8,128)S(1)} %collective-permute-done.14.other_ref, f32[1,256,1024]{2,1,0:T(8,128)S(1)} %get-tuple-element.57.mt_ref, ...), custom_call_target="tpu_custom_call", output_to_operand_aliasing={{0}: (3, {}), {1}: (4, {})} | custom-call | flops 805306368 | bytes 2097152 | tf_op jit(solution)/shard_map/pallas_call | solution.py:356
  (17 shorter events, 0.3 us)
Async XLA Ops:
  0.6 0.7 copy-start
  1.3 38.4 %copy-start.1 = (f32[1024]{0:T(1024)S(1)}, f32[1024]{0:T(1024)}, u32[]{:S(2)}) copy-start(f32[1024]{0:T(1024)} %param.4) | copy-start | bytes 12292
  11.6 16.2 %collective-permute-start.6 = (f32[2,2,32,1024]{3,2,1,0:T(8,128)S(1)}, f32[2,2,32,1024]{3,2,1,0:T(8,128)S(1)}, u32[]{:S(2)}, u32[]{:S(2)}) collective-permute-start(f32[2,2,32,1024]{3,2,1,0:T(8,128)S(1)} %get-tuple-element.52), channel_id=1, source_target_pairs={{0,64},{32,96},{64,0},{96,32},{1,65},{33,97},{65,1},{97,33},{2,66}... | collective-permute-start | bytes 1572872 | tf_op jit(solution)/shard_map/ppermute | solution.py:389
  16.1 23.4 %collective-permute-start.3 = (f32[2,2,32,1024]{3,2,1,0:T(8,128)S(1)}, f32[2,2,32,1024]{3,2,1,0:T(8,128)S(1)}, u32[]{:S(2)}, u32[]{:S(2)}) collective-permute-start(f32[2,2,32,1024]{3,2,1,0:T(8,128)S(1)} %get-tuple-element.47), channel_id=1, source_target_pairs={{0,96},{32,0},{64,32},{96,64},{1,97},{33,1},{65,33},{97,65},{2,98}... | collective-permute-start | bytes 1572872 | tf_op jit(solution)/shard_map/ppermute | solution.py:389
  16.5 23.2 %collective-permute-start = (f32[2,2,32,1024]{3,2,1,0:T(8,128)S(1)}, f32[2,2,32,1024]{3,2,1,0:T(8,128)S(1)}, u32[]{:S(2)}, u32[]{:S(2)}) collective-permute-start(f32[2,2,32,1024]{3,2,1,0:T(8,128)S(1)} %get-tuple-element.42), channel_id=1, source_target_pairs={{0,32},{32,64},{64,96},{96,0},{1,33},{33,65},{65,97},{97,1},{2,34}... | collective-permute-start | bytes 1572872 | tf_op jit(solution)/shard_map/ppermute | solution.py:389
  41.2 2.4 %collective-permute-start.21 = (f32[3,128,128]{2,1,0:T(8,128)S(1)}, f32[3,128,128]{2,1,0:T(8,128)S(1)}, u32[]{:S(2)}, u32[]{:S(2)}) collective-permute-start(f32[3,128,128]{2,1,0:T(8,128)S(1)} %get-tuple-element.70), channel_id=1, source_target_pairs={{0,1},{1,0},{2,3},{3,2},{4,5},{5,4},{6,7},{7,6},{8,9},{9,8},{10,11... | collective-permute-start | bytes 589832 | tf_op jit(solution)/shard_map/ppermute | solution.py:183
  43.6 4.9 %collective-permute-start.22 = (f32[3,128,128]{2,1,0:T(8,128)S(1)}, f32[3,128,128]{2,1,0:T(8,128)S(1)}, u32[]{:S(2)}, u32[]{:S(2)}) collective-permute-start(f32[3,128,128]{2,1,0:T(8,128)S(1)} %add.55), channel_id=1, source_target_pairs={{0,2},{1,9},{2,0},{3,11},{4,6},{5,13},{6,4},{7,15},{8,10},{9,1},{1... | collective-permute-start | bytes 589832 | tf_op jit(solution)/shard_map/ppermute | solution.py:183
  48.6 6.5 %collective-permute-start.23 = (f32[3,128,128]{2,1,0:T(8,128)S(1)}, f32[3,128,128]{2,1,0:T(8,128)S(1)}, u32[]{:S(2)}, u32[]{:S(2)}) collective-permute-start(f32[3,128,128]{2,1,0:T(8,128)S(1)} %add.56), channel_id=1, source_target_pairs={{0,6},{1,25},{2,4},{3,27},{4,2},{5,29},{6,0},{7,31},{8,14},{9,17},... | collective-permute-start | bytes 589832 | tf_op jit(solution)/shard_map/ppermute | solution.py:183
  51.4 8.1 %collective-permute-start.7 = (f32[1,2,32,1024]{3,2,1,0:T(8,128)S(1)}, f32[1,2,32,1024]{3,2,1,0:T(8,128)S(1)}, u32[]{:S(2)}, u32[]{:S(2)}) collective-permute-start(f32[1,2,32,1024]{3,2,1,0:T(8,128)S(1)} %get-tuple-element.53), channel_id=1, source_target_pairs={{0,64},{32,96},{64,0},{96,32},{1,65},{33,97},{65,1},{97,33},{2,66}... | collective-permute-start | bytes 786440 | tf_op jit(solution)/shard_map/ppermute | solution.py:389
  53.6 12.1 %collective-permute-start.4 = (f32[1,2,32,1024]{3,2,1,0:T(8,128)S(1)}, f32[1,2,32,1024]{3,2,1,0:T(8,128)S(1)}, u32[]{:S(2)}, u32[]{:S(2)}) collective-permute-start(f32[1,2,32,1024]{3,2,1,0:T(8,128)S(1)} %get-tuple-element.48), channel_id=1, source_target_pairs={{0,96},{32,0},{64,32},{96,64},{1,97},{33,1},{65,33},{97,65},{2,98}... | collective-permute-start | bytes 786440 | tf_op jit(solution)/shard_map/ppermute | solution.py:389
  54.5 11.6 %collective-permute-start.1 = (f32[1,2,32,1024]{3,2,1,0:T(8,128)S(1)}, f32[1,2,32,1024]{3,2,1,0:T(8,128)S(1)}, u32[]{:S(2)}, u32[]{:S(2)}) collective-permute-start(f32[1,2,32,1024]{3,2,1,0:T(8,128)S(1)} %get-tuple-element.43), channel_id=1, source_target_pairs={{0,32},{32,64},{64,96},{96,0},{1,33},{33,65},{65,97},{97,1},{2,34}... | collective-permute-start | bytes 786440 | tf_op jit(solution)/shard_map/ppermute | solution.py:389
  55.1 15.3 %collective-permute-start.24 = (f32[3,128,128]{2,1,0:T(8,128)S(1)}, f32[3,128,128]{2,1,0:T(8,128)S(1)}, u32[]{:S(2)}, u32[]{:S(2)}) collective-permute-start(f32[3,128,128]{2,1,0:T(8,128)S(1)} %add.57), channel_id=1, source_target_pairs={{0,8},{1,3},{2,10},{3,1},{4,12},{5,7},{6,14},{7,5},{8,0},{9,11},{1... | collective-permute-start | bytes 589832 | tf_op jit(solution)/shard_map/ppermute | solution.py:183
  66.1 20.4 %collective-permute-start.8 = (f32[1,2,32,1024]{3,2,1,0:T(8,128)S(1)}, f32[1,2,32,1024]{3,2,1,0:T(8,128)S(1)}, u32[]{:S(2)}, u32[]{:S(2)}) collective-permute-start(f32[1,2,32,1024]{3,2,1,0:T(8,128)S(1)} %get-tuple-element.54), channel_id=1, source_target_pairs={{0,64},{32,96},{64,0},{96,32},{1,65},{33,97},{65,1},{97,33},{2,66}... | collective-permute-start | bytes 786440 | tf_op jit(solution)/shard_map/ppermute | solution.py:389
  68.9 17.6 %collective-permute-start.5 = (f32[1,2,32,1024]{3,2,1,0:T(8,128)S(1)}, f32[1,2,32,1024]{3,2,1,0:T(8,128)S(1)}, u32[]{:S(2)}, u32[]{:S(2)}) collective-permute-start(f32[1,2,32,1024]{3,2,1,0:T(8,128)S(1)} %get-tuple-element.49), channel_id=1, source_target_pairs={{0,96},{32,0},{64,32},{96,64},{1,97},{33,1},{65,33},{97,65},{2,98}... | collective-permute-start | bytes 786440 | tf_op jit(solution)/shard_map/ppermute | solution.py:389
  69.8 16.7 %collective-permute-start.2 = (f32[1,2,32,1024]{3,2,1,0:T(8,128)S(1)}, f32[1,2,32,1024]{3,2,1,0:T(8,128)S(1)}, u32[]{:S(2)}, u32[]{:S(2)}) collective-permute-start(f32[1,2,32,1024]{3,2,1,0:T(8,128)S(1)} %get-tuple-element.44), channel_id=1, source_target_pairs={{0,32},{32,64},{64,96},{96,0},{1,33},{33,65},{65,97},{97,1},{2,34}... | collective-permute-start | bytes 786440 | tf_op jit(solution)/shard_map/ppermute | solution.py:389
  70.4 6.1 %collective-permute-start.25 = (f32[3,128,128]{2,1,0:T(8,128)S(1)}, f32[3,128,128]{2,1,0:T(8,128)S(1)}, u32[]{:S(2)}, u32[]{:S(2)}) collective-permute-start(f32[3,128,128]{2,1,0:T(8,128)S(1)} %add.58), channel_id=1, source_target_pairs={{0,24},{1,7},{2,26},{3,5},{4,28},{5,3},{6,30},{7,1},{8,16},{9,15},... | collective-permute-start | bytes 589832 | tf_op jit(solution)/shard_map/ppermute | solution.py:183
  73.3 14.2 %collective-permute-start.15 = (f32[3,64,128]{2,1,0:T(8,128)S(1)}, f32[3,64,128]{2,1,0:T(8,128)S(1)}, u32[]{:S(2)}, u32[]{:S(2)}) collective-permute-start(f32[3,64,128]{2,1,0:T(8,128)S(1)} %get-tuple-element.63), channel_id=1, source_target_pairs={{0,1},{1,0},{2,3},{3,2},{4,5},{5,4},{6,7},{7,6},{8,9},{9,8},{10,11... | collective-permute-start | bytes 294920 | tf_op jit(solution)/shard_map/ppermute | solution.py:183
  84.3 27.5 %collective-permute-start.26 = (f32[2,256,256]{2,1,0:T(8,128)S(1)}, f32[2,256,256]{2,1,0:T(8,128)S(1)}, u32[]{:S(2)}, u32[]{:S(2)}) collective-permute-start(f32[2,256,256]{2,1,0:T(8,128)S(1)} %shard_map.54.mine_ref), channel_id=1, source_target_pairs={{0,1},{1,0},{2,3},{3,2},{4,5},{5,4},{6,7},{7,6},{8,9},{9,8},{10,11... | collective-permute-start | bytes 1572872 | tf_op jit(solution)/shard_map/ppermute | solution.py:183
  87.3 1.4 %collective-permute-start.9 = (f32[3,64,128]{2,1,0:T(8,128)S(1)}, f32[3,64,128]{2,1,0:T(8,128)S(1)}, u32[]{:S(2)}, u32[]{:S(2)}) collective-permute-start(f32[3,64,128]{2,1,0:T(8,128)S(1)} %get-tuple-element.56), channel_id=1, source_target_pairs={{0,1},{1,0},{2,3},{3,2},{4,5},{5,4},{6,7},{7,6},{8,9},{9,8},{10,11... | collective-permute-start | bytes 294920 | tf_op jit(solution)/shard_map/ppermute | solution.py:183
  87.5 3.8 %collective-permute-start.16 = (f32[3,64,128]{2,1,0:T(8,128)S(1)}, f32[3,64,128]{2,1,0:T(8,128)S(1)}, u32[]{:S(2)}, u32[]{:S(2)}) collective-permute-start(f32[3,64,128]{2,1,0:T(8,128)S(1)} %add.50), channel_id=1, source_target_pairs={{0,2},{1,9},{2,0},{3,11},{4,6},{5,13},{6,4},{7,15},{8,10},{9,1},{1... | collective-permute-start | bytes 294920 | tf_op jit(solution)/shard_map/ppermute | solution.py:183
  88.7 3.5 %collective-permute-start.10 = (f32[3,64,128]{2,1,0:T(8,128)S(1)}, f32[3,64,128]{2,1,0:T(8,128)S(1)}, u32[]{:S(2)}, u32[]{:S(2)}) collective-permute-start(f32[3,64,128]{2,1,0:T(8,128)S(1)} %add.45), channel_id=1, source_target_pairs={{0,2},{1,9},{2,0},{3,11},{4,6},{5,13},{6,4},{7,15},{8,10},{9,1},{1... | collective-permute-start | bytes 294920 | tf_op jit(solution)/shard_map/ppermute | solution.py:183
  91.3 4.8 %collective-permute-start.17 = (f32[3,64,128]{2,1,0:T(8,128)S(1)}, f32[3,64,128]{2,1,0:T(8,128)S(1)}, u32[]{:S(2)}, u32[]{:S(2)}) collective-permute-start(f32[3,64,128]{2,1,0:T(8,128)S(1)} %add.51), channel_id=1, source_target_pairs={{0,6},{1,25},{2,4},{3,27},{4,2},{5,29},{6,0},{7,31},{8,14},{9,17},... | collective-permute-start | bytes 294920 | tf_op jit(solution)/shard_map/ppermute | solution.py:183
  92.3 5.1 %collective-permute-start.11 = (f32[3,64,128]{2,1,0:T(8,128)S(1)}, f32[3,64,128]{2,1,0:T(8,128)S(1)}, u32[]{:S(2)}, u32[]{:S(2)}) collective-permute-start(f32[3,64,128]{2,1,0:T(8,128)S(1)} %add.46), channel_id=1, source_target_pairs={{0,6},{1,25},{2,4},{3,27},{4,2},{5,29},{6,0},{7,31},{8,14},{9,17},... | collective-permute-start | bytes 294920 | tf_op jit(solution)/shard_map/ppermute | solution.py:183
  96.1 3.8 %collective-permute-start.18 = (f32[3,64,128]{2,1,0:T(8,128)S(1)}, f32[3,64,128]{2,1,0:T(8,128)S(1)}, u32[]{:S(2)}, u32[]{:S(2)}) collective-permute-start(f32[3,64,128]{2,1,0:T(8,128)S(1)} %add.52), channel_id=1, source_target_pairs={{0,8},{1,3},{2,10},{3,1},{4,12},{5,7},{6,14},{7,5},{8,0},{9,11},{1... | collective-permute-start | bytes 294920 | tf_op jit(solution)/shard_map/ppermute | solution.py:183
  97.5 4.2 %collective-permute-start.12 = (f32[3,64,128]{2,1,0:T(8,128)S(1)}, f32[3,64,128]{2,1,0:T(8,128)S(1)}, u32[]{:S(2)}, u32[]{:S(2)}) collective-permute-start(f32[3,64,128]{2,1,0:T(8,128)S(1)} %add.47), channel_id=1, source_target_pairs={{0,8},{1,3},{2,10},{3,1},{4,12},{5,7},{6,14},{7,5},{8,0},{9,11},{1... | collective-permute-start | bytes 294920 | tf_op jit(solution)/shard_map/ppermute | solution.py:183
  100.0 4.8 %collective-permute-start.19 = (f32[3,64,128]{2,1,0:T(8,128)S(1)}, f32[3,64,128]{2,1,0:T(8,128)S(1)}, u32[]{:S(2)}, u32[]{:S(2)}) collective-permute-start(f32[3,64,128]{2,1,0:T(8,128)S(1)} %add.53), channel_id=1, source_target_pairs={{0,24},{1,7},{2,26},{3,5},{4,28},{5,3},{6,30},{7,1},{8,16},{9,15},... | collective-permute-start | bytes 294920 | tf_op jit(solution)/shard_map/ppermute | solution.py:183
  101.7 7.6 %collective-permute-start.13 = (f32[3,64,128]{2,1,0:T(8,128)S(1)}, f32[3,64,128]{2,1,0:T(8,128)S(1)}, u32[]{:S(2)}, u32[]{:S(2)}) collective-permute-start(f32[3,64,128]{2,1,0:T(8,128)S(1)} %add.48), channel_id=1, source_target_pairs={{0,24},{1,7},{2,26},{3,5},{4,28},{5,3},{6,30},{7,1},{8,16},{9,15},... | collective-permute-start | bytes 294920 | tf_op jit(solution)/shard_map/ppermute | solution.py:183
  104.7 10.2 %collective-permute-start.20 = (f32[3,64,128]{2,1,0:T(8,128)S(1)}, f32[3,64,128]{2,1,0:T(8,128)S(1)}, u32[]{:S(2)}, u32[]{:S(2)}) collective-permute-start(f32[3,64,128]{2,1,0:T(8,128)S(1)} %add.54.mine_ref), channel_id=1, source_target_pairs={{0,1},{1,0},{2,3},{3,2},{4,5},{5,4},{6,7},{7,6},{8,9},{9,8},{10,11... | collective-permute-start | bytes 294920 | tf_op jit(solution)/shard_map/ppermute | solution.py:183
  109.3 16.0 %collective-permute-start.14 = (f32[3,64,128]{2,1,0:T(8,128)S(1)}, f32[3,64,128]{2,1,0:T(8,128)S(1)}, u32[]{:S(2)}, u32[]{:S(2)}) collective-permute-start(f32[3,64,128]{2,1,0:T(8,128)S(1)} %add.49.mine_ref), channel_id=1, source_target_pairs={{0,1},{1,0},{2,3},{3,2},{4,5},{5,4},{6,7},{7,6},{8,9},{9,8},{10,11... | collective-permute-start | bytes 294920 | tf_op jit(solution)/shard_map/ppermute | solution.py:183

commit v2 on v0

v2 whole, which is shorter than its diff:
```python
import functools
import math

import jax
import jax.numpy as jnp
from jax import lax
from jax.experimental import pallas as pl
from jax.experimental.pallas import tpu as pltpu
from jax.sharding import PartitionSpec as P

HIGHEST = lax.Precision.HIGHEST
HOPS = (0, 1, 3, 2)
GROUPS = ((0, 1), (2, 3))
PANEL = 32
CUTS = (4,)
STEPS = (0, 1, 2, 3)
EARLY = 2
IN_VMEM = pl.BlockSpec(memory_space=pltpu.VMEM)
IN_HBM = pl.BlockSpec(memory_space=pltpu.HBM)
SMALL = pl.CostEstimate(flops=1000, bytes_accessed=1000, transcendentals=0)


def dot(a, b, dims, precision=None):
    return lax.dot_general(
        a, b, (dims, ((), ())), precision=precision, preferred_element_type=jnp.float32
    )


def dot3(a, b, dims):
    ah, bh = a.astype(jnp.bfloat16), b.astype(jnp.bfloat16)
    al = (a - ah.astype(jnp.float32)).astype(jnp.bfloat16)
    bl = (b - bh.astype(jnp.float32)).astype(jnp.bfloat16)
    return dot(ah, bh, dims) + (dot(ah, bl, dims) + dot(al, bh, dims))


def transform_kernel(bins_in, seg_ref, *refs):
    outs, (table, landing, held, sems, bins_ref, bins_sem) = refs[:-6], refs[-6:]
    n_seg, fft_len = seg_ref.shape[0], seg_ref.shape[1]
    group, n_rows = 8, table.shape[0]
    per_hop = n_rows // len(HOPS)
    n_local = per_hop // 2

    batch = 4

    def segment_copy(b):
        some = pl.ds(b * batch, batch)
        return pltpu.make_async_copy(seg_ref.at[some], held.at[some], sems.at[b])

    bins_copy = pltpu.make_async_copy(bins_in, bins_ref, bins_sem)
    bins_copy.start()
    for b in range(n_seg // batch):
        segment_copy(b).start()
    me = lax.axis_index("freq")
    row = lax.broadcasted_iota(jnp.int32, (n_rows, fft_len), 0)
    step = lax.broadcasted_iota(jnp.int32, (n_rows, fft_len), 1)
    bins = jnp.zeros((n_rows, fft_len), jnp.int32)
    bins_copy.wait()
    for h, hop in enumerate(HOPS):
        home = lax.rem(me + hop, len(HOPS))
        for j in range(n_local):
            which = bins_ref[home * n_local + j]
            bins = jnp.where(row // 2 == h * n_local + j, which, bins)
    phase = lax.rem(bins * step, fft_len)
    angle = 2.0 * math.pi / fft_len * phase.astype(jnp.float32)
    window = 0.5 - 0.5 * jnp.cos(2.0 * math.pi / fft_len * step.astype(jnp.float32))
    scale = window / math.sqrt(fft_len)
    wave = jnp.where(lax.rem(row, 2) == 0, jnp.cos(angle), -jnp.sin(angle))
    table[...] = (scale * wave).astype(jnp.bfloat16)

    @pl.loop(0, n_seg // group)
    def _(g):
        base = pl.multiple_of(g * group, group)
        for b in range(group):
            if b % batch == 0:
                segment_copy(g * (group // batch) + b // batch).wait()
            sums = dot(table[...], held[base + b], ((1,), (0,)))
            for k in range(landing.shape[0]):
                tile = slice(128 * k, 128 * k + 128)
                landing[k, pl.ds(b, n_rows, stride=group), :] = sums[:, tile]
        n = 0
        for js in GROUPS:
            for h in range(len(HOPS)):
                for i, j in enumerate(js):
                    for c in range(2):
                        r = (h * per_hop + j * 2 + c) * group
                        for k in range(landing.shape[0]):
                            tile = slice(128 * k, 128 * k + 128)
                            outs[n][i, c, pl.ds(base, group), tile] = landing[k, r : r + group, :]
                n += 1


def transform(bins, segments):
    n_seg, fft_len, n_x = segments.shape
    n_rows = 2 * bins.shape[0]
    shapes = [
        jax.ShapeDtypeStruct((len(js), 2, n_seg, n_x), jnp.float32)
        for js in GROUPS
        for _ in HOPS
    ]
    outs = pl.pallas_call(
        transform_kernel,
        out_shape=shapes,
        in_specs=[IN_HBM, IN_HBM],
        out_specs=[IN_VMEM] * len(shapes),
        scratch_shapes=[
            pltpu.VMEM((n_rows, fft_len), jnp.bfloat16),
            pltpu.VMEM((n_x // 128, n_rows * 8, 128), jnp.float32),
            pltpu.VMEM(segments.shape, segments.dtype),
            pltpu.SemaphoreType.DMA((n_seg,)),
            pltpu.SMEM(bins.shape, bins.dtype),
            pltpu.SemaphoreType.DMA,
        ],
        compiler_params=pltpu.CompilerParams(vmem_limit_bytes=50 << 20),
        cost_estimate=SMALL,
    )(bins, segments)
    k = len(HOPS)
    return [outs[i * k : (i + 1) * k] for i in range(len(GROUPS))]


def gram_kernel(vol_ref, *refs):
    pieces, (mt_ref, mine_ref, other_ref, packed) = refs[:4], refs[4:]
    me, core = lax.axis_index("freq"), lax.rem(lax.axis_index("space"), 2)
    n_seg = pieces[0].shape[2]
    n_all = n_seg * len(HOPS)
    row = lax.broadcasted_iota(jnp.int32, (n_all, n_all), 0)
    col = lax.broadcasted_iota(jnp.int32, (n_all, n_all), 1)
    for j in range(mt_ref.shape[0]):
        for h, hop in enumerate(HOPS):
            source = lax.rem(me + len(HOPS) - hop, len(HOPS))
            for c in range(2):
                start = pl.multiple_of(c * n_all + source * n_seg, n_seg)
                mt_ref[j, pl.ds(start, n_seg), :] = pieces[h][j, c]
        m = mt_ref[j]
        g = dot3(m, m * vol_ref[...], ((1,), (1,)))
        g11, g21, g22 = g[:n_all, :n_all], g[n_all:, :n_all], g[n_all:, n_all:]
        packed[j, :n_all, :] = g21
        packed[j, n_all : 2 * n_all, :] = jnp.where(row >= col, g11, g22)
        diagonal = jnp.sum(jnp.where(row == col, g22, 0.0), axis=0, keepdims=True)
        packed[j, 2 * n_all :, :] = jnp.broadcast_to(diagonal, (8, n_all))
    mine_ref[...] = packed[core]
    other_ref[...] = packed[1 - core]


def gram(volumes, pieces):
    nj, two, n_seg, n_x = pieces[0].shape
    n = two * n_seg * len(HOPS)
    part = (n + 8, n // 2)
    return pl.pallas_call(
        gram_kernel,
        out_shape=[
            jax.ShapeDtypeStruct((nj, n, n_x), jnp.float32),
            jax.ShapeDtypeStruct(part, jnp.float32),
            jax.ShapeDtypeStruct(part, jnp.float32),
        ],
        in_specs=[IN_VMEM] * (1 + len(HOPS)),
        out_specs=[IN_VMEM] * 3,
        scratch_shapes=[pltpu.VMEM((nj,) + part, jnp.float32)],
        compiler_params=pltpu.CompilerParams(vmem_limit_bytes=16 << 20),
        cost_estimate=SMALL,
    )(volumes.reshape(1, n_x), *pieces)


def space_pairs(kind):
    pairs = []
    for i in range(32):
        y, x, core = i // 8, i // 2 % 4, i % 2
        if kind == "core":
            core = 1 - core
        else:
            along_x = (kind < 2) == (core == 0)
            flip = (lambda v: v ^ 1) if kind % 2 == 0 else (lambda v: 3 - v)
            x, y = (flip(x), y) if along_x else (x, flip(y))
        pairs.append((i, (y * 4 + x) * 2 + core))
    return pairs


def swap(value, kind):
    return lax.ppermute(value, "space", space_pairs(kind))


def add_steps(value, steps):
    for kind in steps:
        value = value + swap(value, kind)
    return value


def factor(work, begin, end):
    n = work.shape[0]
    rows = lax.broadcasted_iota(jnp.int32, (8, 128), 0)
    n_sub, half = PANEL // 8, n // 128
    for base in range(begin * PANEL, end * PANEL, PANEL):
        tile, lane = base // 128, base % 128
        tiles = [
            t for t in range(2 * half)
            if (tile <= t < half) or (t >= half and (t - half) * 128 < base + PANEL)
        ]
        live = [
            {t: work[base + 8 * i : base + 8 * i + 8, 128 * t : 128 * t + 128] for t in tiles}
            for i in range(n_sub)
        ]
        done = [{} for _ in range(n_sub)]
        column = [
            {
                j: jnp.broadcast_to(live[i][tile][:, lane + j : lane + j + 1], (8, 128))
                for j in range(8 * i + 8)
            }
            for i in range(n_sub)
        ]
        for p in range(PANEL):
            ip, sp = p // 8, p % 8
            pivot = jnp.broadcast_to(column[ip][p][sp : sp + 1, :], (8, 128))
            root = lax.rsqrt(pivot)
            inv = root * root
            mult = {i: column[i][p] * inv for i in range(ip, n_sub)}
            for j in range(p + 1, PANEL):
                ij = j // 8
                entry = jnp.broadcast_to(column[ij][p][j % 8 : j % 8 + 1, :], (8, 128))
                for i in range(ij, n_sub):
                    column[i][j] = column[i][j] - mult[i] * entry
            for t in tiles:
                row = jnp.broadcast_to(live[ip][t][sp : sp + 1, :], (8, 128))
                scaled = row * root
                done[ip][t] = scaled if sp == 0 else jnp.where(rows == sp, scaled, done[ip][t])
                for i in range(ip, n_sub):
                    if i > ip or sp < 7:
                        live[i][t] = live[i][t] - mult[i] * row
        for i in range(n_sub):
            for t in tiles:
                work[base + 8 * i : base + 8 * i + 8, 128 * t : 128 * t + 128] = done[i][t]
        after = base + PANEL
        first = after // 128
        for blk in range(first, half):
            lo, hi = max(after, 128 * blk), 128 * blk + 128
            left = work[base:after, 128 * blk : hi]
            for c0, c1 in ((128 * first, n), (n, n + (after + 127) // 128 * 128)):
                right = work[base:after, c0:c1]
                update = dot(left, right, ((0,), (0,)), HIGHEST)
                work[lo:hi, c0:c1] = work[lo:hi, c0:c1] - update[lo - 128 * blk :, :]


def load_gram(work, packed):
    n = work.shape[0]
    h = n // 2
    row = lax.broadcasted_iota(jnp.int32, (h, h), 0)
    col = lax.broadcasted_iota(jnp.int32, (h, h), 1)
    g21, square = packed[:h, :], packed[h:n, :]
    turned = square.T
    work[:h, :h] = jnp.where(row >= col, square, turned)
    work[:h, h:n] = g21.T
    work[h:, :h] = g21
    g22 = jnp.where(row < col, square, turned)
    work[h:, h:n] = jnp.where(row == col, packed[n : n + 1, :], g22)
    row = lax.broadcasted_iota(jnp.int32, (n, n), 0)
    col = lax.broadcasted_iota(jnp.int32, (n, n), 1)
    work[:, n:] = jnp.where(row == col, 1.0, 0.0)


def factor_kernel(begin, end, in_ref, out_ref, work):
    n = work.shape[0]
    if begin == 0:
        load_gram(work, in_ref)
    else:
        work[...] = in_ref[...]
    factor(work, begin, end)
    if end * PANEL < n:
        out_ref[...] = work[...]
    else:
        row = lax.broadcasted_iota(jnp.int32, (n, n), 0)
        col = lax.broadcasted_iota(jnp.int32, (n, n), 1)
        out_ref[0] = jnp.where(row <= col, work[:, :n], 0.0)
        out_ref[1] = jnp.where(row >= col, work[:, n:], 0.0)


def factor_call(value, cuts):
    n = 2 * value.shape[1]
    ends = tuple(cuts) + (n // PANEL,)
    for begin, end in zip((0,) + ends, ends):
        last = end * PANEL == n
        value = pl.pallas_call(
            functools.partial(factor_kernel, begin, end),
            out_shape=jax.ShapeDtypeStruct((2, n, n) if last else (n, 2 * n), jnp.float32),
            in_specs=[IN_VMEM],
            out_specs=IN_VMEM,
            scratch_shapes=[pltpu.VMEM((n, 2 * n), jnp.float32)],
            compiler_params=pltpu.CompilerParams(vmem_limit_bytes=8 << 20),
            cost_estimate=pl.CostEstimate(
                flops=(end - begin) << 29, bytes_accessed=1000, transcendentals=0
            ),
        )(value)
    return value


def modes_kernel(js, root_rows, mine_ref, other_ref, mt_ref, *refs):
    modes_ref, tri_ref, inverse, held, tri, sems, tri_sems = refs[-7:]
    core = lax.rem(lax.axis_index("space"), 2)
    n_parts, part = held.shape[1], held.shape[2]

    def tri_copy(i):
        return pltpu.make_async_copy(tri.at[i], tri_ref.at[js[i]], tri_sems.at[i])

    def modes_copy(i, q):
        rows = pl.ds(q * part, part)
        return pltpu.make_async_copy(held.at[i, q], modes_ref.at[js[i], rows, :], sems.at[i, q])

    for i in range(len(js)):

        @pl.when(core == i)
        def _():
            tri[i] = mine_ref[0] * (1.0 / root_rows)
            inverse[i] = mine_ref[1] * root_rows

        @pl.when(core != i)
        def _():
            tri[i] = other_ref[0] * (1.0 / root_rows)
            inverse[i] = other_ref[1] * root_rows

        tri_copy(i).start()
    for i in range(len(js)):
        for q in range(n_parts):
            rows = slice(q * part, q * part + part)
            held[i, q] = dot3(mt_ref[i, :, rows], inverse[i], ((0,), (1,)))
            modes_copy(i, q).start()
    for i in range(len(js)):
        tri_copy(i).wait()
        for q in range(n_parts):
            modes_copy(i, q).wait()


def modes_call(js, n_local, root_rows, mine, other, mt, before):
    nj, n, n_x = mt.shape
    parts = 4
    before = list(before)
    return pl.pallas_call(
        functools.partial(modes_kernel, js, root_rows),
        out_shape=[
            jax.ShapeDtypeStruct((n_local, n_x, n), jnp.float32),
            jax.ShapeDtypeStruct((n_local, n, n), jnp.float32),
        ],
        in_specs=[IN_VMEM] * 3 + [IN_HBM] * len(before),
        out_specs=[IN_HBM, IN_HBM],
        scratch_shapes=[
            pltpu.VMEM((nj, n, n), jnp.float32),
            pltpu.VMEM((nj, parts, n_x // parts, n), jnp.float32),
            pltpu.VMEM((nj, n, n), jnp.float32),
            pltpu.SemaphoreType.DMA((nj, parts)),
            pltpu.SemaphoreType.DMA((nj,)),
        ],
        input_output_aliases={3 + i: i for i in range(len(before))},
        compiler_params=pltpu.CompilerParams(vmem_limit_bytes=16 << 20),
        cost_estimate=SMALL,
    )(mine, other, mt, *before)


def on_device(segments, volumes, freq_bins):
    n_freq = lax.axis_size("freq")
    n_local = freq_bins.shape[0] // n_freq
    root_rows = math.sqrt(segments.shape[2] * lax.axis_size("space"))
    sent = transform(freq_bins, segments)
    arrived = []
    for pieces in sent:
        got = [pieces[0]]
        for h, hop in enumerate(HOPS):
            if hop == 0:
                continue
            piece = pieces[h]
            if arrived:
                piece, arrived[-1][h] = lax.optimization_barrier((piece, arrived[-1][h]))
            got.append(lax.ppermute(piece, "freq", [(i, (i + hop) % n_freq) for i in range(n_freq)]))
        arrived.append(got)
    sums = []
    for got in arrived:
        mt, mine, other = gram(volumes, got)
        value = add_steps(mine + swap(other, "core"), STEPS[:EARLY])
        value, volumes = lax.optimization_barrier((value, volumes))
        sums.append((mt, value))
    outs = ()
    for js, (mt, value) in zip(GROUPS, sums):
        value = factor_call(add_steps(value, STEPS[EARLY:]), CUTS if js[0] == 0 else ())
        outs = modes_call(js, n_local, root_rows, value, swap(value, "core"), mt, outs)
    return tuple(outs)


def solution(mesh):
    placed = (P("freq", None, "space"), P("space"), P())
    return jax.shard_map(
        on_device,
        mesh=mesh,
        in_specs=placed,
        out_specs=(P("freq", "space", None), P("freq", None, None)),
        check_vma=False,
    )
```

time: 433 us -> 102 us (0.24)
  other arithmetic: 218 us -> 0.19 us
  waiting for transfers between devices: 105 us -> 35.7 us
  blocking collectives: 53.5 us -> 0 us
  starting transfers between devices: 0.04 us -> 34.1 us
  Pallas kernels: 0 us -> 30.6 us
  matrix products: 22.7 us -> 0 us
  local copies, waits for them, and re-layouts: 18.7 us -> 0.65 us
  between operations: 14.2 us -> 0.91 us
    another operation x14 -> x0, other arithmetic: 214 us -> none  [the longest x10 134 us: on_device(): lower_tri = jnp.linalg.cholesky(gram_sum)]
    psum x1 -> x0, waiting for transfers between devices: 105 us -> none  [on_device(): gram_sum = lax.psum(gram, 'space')]
    all_to_all x1 -> x0, blocking collectives: 53.5 us -> none  [on_device(): lax.all_to_all(coefficients, 'freq', split_axis=0, concat_axis=3, tiled=T...]
    ppermute x0 -> x18, waiting for transfers between devices: none -> 35.7 us  [the longest x6 24.3 us: on_device(): lax.ppermute(piece, 'freq', [(i, (i + hop) % n_freq) for i in range(n_fre...]
    ppermute x0 -> x18, starting transfers between devices: none -> 34.1 us  [the longest x12 24.7 us: swap(): return lax.ppermute(value, 'space', space_pairs(kind))]
    pallas_call x0 -> x8, Pallas kernels: none -> 30.6 us  [the longest x3 15.6 us: factor_call(): pl.pallas_call(functools.partial(factor_kernel, begin, end), out_shape=ja...]
    dot_general x2 -> x0, matrix products: 14.1 us -> none  [the longest x1 8.79 us: on_device(): jnp.einsum('cft,btx->fxcb', dft_table, segments, preferred_element_type=j...]
    another operation x5 -> x0, matrix products: 8.58 us -> none  [the longest x3 7.53 us: on_device(): basis_t = jax.vmap(solve_one)(lower_tri, jnp.swapaxes(matrix, 1, 2))]
  transfers between devices with their start and end apart: 1 -> 18, of which waited for: 1 -> 8; matrix products, arithmetic and copies ran while one was open for 0% -> 0% of each run, Pallas kernels for 0% -> 19%
where the time goes in v2:
time: 102 us
  waiting for transfers between devices  35.7 us (35%)
  starting transfers between devices  34.1 us (33%)
  Pallas kernels  30.6 us (30%)
    ppermute x12, starting transfers between devices, swap(): return lax.ppermute(value, 'space', space_pairs(kind))  24.7 us
    ppermute x6, waiting for transfers between devices, on_device(): lax.ppermute(piece, 'freq', [(i, (i + hop) % n_freq) for i in range(n_fre...  24.3 us
    pallas_call x3, Pallas kernels, factor_call(): pl.pallas_call(functools.partial(factor_kernel, begin, end), out_shape=ja...  15.6 us
    ppermute x12, waiting for transfers between devices, swap(): return lax.ppermute(value, 'space', space_pairs(kind))  11.4 us
    ppermute x6, starting transfers between devices, on_device(): lax.ppermute(piece, 'freq', [(i, (i + hop) % n_freq) for i in range(n_fre...  9.34 us
    pallas_call x1, Pallas kernels, transform(): pl.pallas_call(transform_kernel, out_shape=shapes, in_specs=[IN_HBM, IN_H...  7.51 us
    pallas_call x2, Pallas kernels, modes_call(): pl.pallas_call(functools.partial(modes_kernel, js, root_rows), out_shape=...  4.14 us
    pallas_call x2, Pallas kernels, gram(): pl.pallas_call(gram_kernel, out_shape=[jax.ShapeDtypeStruct((nj, n, n_x),...  3.35 us
  transfers between devices with their start and end apart: 18, of which 8 were waited for; matrix products, arithmetic and copies ran while one was open for 0% of the time, Pallas kernels for 19%

profile of v2, /device:TPU:1, one launch (start us, length us, event | category | flops | bytes accessed | tf_op | source)
XLA Modules:
  0.0 102.1 jit_solution(1904934087340835829)
XLA Ops:
  0.6 0.0 copy-start.1
  0.6 0.6 copy-done.1
  1.3 0.0 copy-start
  1.3 7.5 %shard_map.50 = (f32[2,2,32,1024]{3,2,1,0:T(8,128)S(1)}, f32[2,2,32,1024]{3,2,1,0:T(8,128)S(1)}, f32[2,2,32,1024]{3,2,1,0:T(8,128)S(1)}, f32[2,2,32,1024]{3,2,1,...) custom-call(s32[16]{0:T(128)S(1)} %copy-done.1, ...), custom_call_target="tpu_custom_call" | custom-call | flops 1000 | bytes 1000 | tf_op jit(solution)/shard_map/pallas_call | solution.py:100
  8.8 2.5 %collective-permute-start = (f32[2,2,32,1024]{3,2,1,0:T(8,128)S(1)}, f32[2,2,32,1024]{3,2,1,0:T(8,128)S(1)}, u32[]{:S(2)}, u32[]{:S(2)}) collective-permute-start(f32[2,2,32,1024]{3,2,1,0:T(8,128)S(1)} %get-tuple-element.29), channel_id=1, source_target_pairs={{0,32},{32,64},{64,96},{96,0},{1,33},{33,65},{65,97},{97,1},{2,34}... | collective-permute-start | bytes 1572872 | tf_op jit(solution)/shard_map/ppermute | solution.py:368
  11.3 2.2 %collective-permute-start.1 = (f32[2,2,32,1024]{3,2,1,0:T(8,128)S(1)}, f32[2,2,32,1024]{3,2,1,0:T(8,128)S(1)}, u32[]{:S(2)}, u32[]{:S(2)}) collective-permute-start(f32[2,2,32,1024]{3,2,1,0:T(8,128)S(1)} %get-tuple-element.32), channel_id=1, source_target_pairs={{0,96},{32,0},{64,32},{96,64},{1,97},{33,1},{65,33},{97,65},{2,98}... | collective-permute-start | bytes 1572872 | tf_op jit(solution)/shard_map/ppermute | solution.py:368
  13.5 1.2 %collective-permute-start.2 = (f32[2,2,32,1024]{3,2,1,0:T(8,128)S(1)}, f32[2,2,32,1024]{3,2,1,0:T(8,128)S(1)}, u32[]{:S(2)}, u32[]{:S(2)}) collective-permute-start(f32[2,2,32,1024]{3,2,1,0:T(8,128)S(1)} %get-tuple-element.35), channel_id=1, source_target_pairs={{0,64},{32,96},{64,0},{96,32},{1,65},{33,97},{65,1},{97,33},{2,66}... | collective-permute-start | bytes 1572872 | tf_op jit(solution)/shard_map/ppermute | solution.py:368
  14.8 10.3 %collective-permute-done.refs_1_ = f32[2,2,32,1024]{3,2,1,0:T(8,128)S(1)} collective-permute-done((f32[2,2,32,1024]{3,2,1,0:T(8,128)S(1)}, f32[2,2,32,1024]{3,2,1,0:T(8,128)S(1)}, u32[]{:S(2)}, u32[]{:S(2)}) %collective-permute-start) | collective-permute-done | bytes 524320 | tf_op jit(solution)/shard_map/ppermute | solution.py:368
  25.1 0.0 collective-permute-start.6
  25.1 0.0 collective-permute-done.1.refs_2_
  25.1 3.4 %collective-permute-start.7 = (f32[2,2,32,1024]{3,2,1,0:T(8,128)S(1)}, f32[2,2,32,1024]{3,2,1,0:T(8,128)S(1)}, u32[]{:S(2)}, u32[]{:S(2)}) collective-permute-start(f32[2,2,32,1024]{3,2,1,0:T(8,128)S(1)} %get-tuple-element.42), channel_id=1, source_target_pairs={{0,96},{32,0},{64,32},{96,64},{1,97},{33,1},{65,33},{97,65},{2,98}... | collective-permute-start | bytes 1572872 | tf_op jit(solution)/shard_map/ppermute | solution.py:368
  28.5 8.8 %collective-permute-done.2.refs_3_ = f32[2,2,32,1024]{3,2,1,0:T(8,128)S(1)} collective-permute-done((f32[2,2,32,1024]{3,2,1,0:T(8,128)S(1)}, f32[2,2,32,1024]{3,2,1,0:T(8,128)S(1)}, u32[]{:S(2)}, u32[]{:S(2)}) %collective-permute-start.2) | collective-permute-done | bytes 524320 | tf_op jit(solution)/shard_map/ppermute | solution.py:368
  37.2 0.0 collective-permute-start.8
  37.2 0.0 copy-done
  37.3 1.7 %shard_map.51 = (f32[2,256,1024]{2,1,0:T(8,128)S(1)}, f32[264,128]{1,0:T(8,128)S(1)}, f32[264,128]{1,0:T(8,128)S(1)}) custom-call(f32[1,1024]{1,0:T(1,128)S(1)} %bitcast.2, f32[2,2,32,1024]{3,2,1,0:T(8,128)S(1)} %get-tuple-element.27.refs_0_, f32[2,2,32,1024]{3,2,1,0:T(8,128)S(1)} %collective-permute-done.refs_1_, ...), custom_call_target="tpu_custom_call" | custom-call | flops 1000 | bytes 1000 | tf_op jit(solution)/shard_map/pallas_call | solution.py:148
  38.9 4.1 %collective-permute-start.3 = (f32[264,128]{1,0:T(8,128)S(1)}, f32[264,128]{1,0:T(8,128)S(1)}, u32[]{:S(2)}, u32[]{:S(2)}) collective-permute-start(f32[264,128]{1,0:T(8,128)S(1)} %get-tuple-element.38), channel_id=1, source_target_pairs={{0,1},{1,0},{2,3},{3,2},{4,5},{5,4},{6,7},{7,6},{8,9},{9,8},{10,11... | collective-permute-start | bytes 405512 | tf_op jit(solution)/shard_map/ppermute | solution.py:178
  43.1 1.0 collective-permute-done.3
  44.1 1.4 %collective-permute-start.4 = (f32[264,128]{1,0:T(8,128)S(1)}, f32[264,128]{1,0:T(8,128)S(1)}, u32[]{:S(2)}, u32[]{:S(2)}) collective-permute-start(f32[264,128]{1,0:T(8,128)S(1)} %add.30), channel_id=1, source_target_pairs={{0,2},{1,9},{2,0},{3,11},{4,6},{5,13},{6,4},{7,15},{8,10},{9,1},{1... | collective-permute-start | bytes 405512 | tf_op jit(solution)/shard_map/ppermute | solution.py:178
  45.4 2.9 %collective-permute-done.4 = f32[264,128]{1,0:T(8,128)S(1)} collective-permute-done((f32[264,128]{1,0:T(8,128)S(1)}, f32[264,128]{1,0:T(8,128)S(1)}, u32[]{:S(2)}, u32[]{:S(2)}) %collective-permute-start.4) | collective-permute-done | bytes 135200 | tf_op jit(solution)/shard_map/ppermute | solution.py:178
  48.3 2.8 %collective-permute-start.5 = (f32[264,128]{1,0:T(8,128)S(1)}, f32[264,128]{1,0:T(8,128)S(1)}, u32[]{:S(2)}, u32[]{:S(2)}) collective-permute-start(f32[264,128]{1,0:T(8,128)S(1)} %add.31), channel_id=1, source_target_pairs={{0,6},{1,25},{2,4},{3,27},{4,2},{5,29},{6,0},{7,31},{8,14},{9,17},... | collective-permute-start | bytes 405512 | tf_op jit(solution)/shard_map/ppermute | solution.py:178
  51.1 2.7 %collective-permute-done.5 = f32[264,128]{1,0:T(8,128)S(1)} collective-permute-done((f32[264,128]{1,0:T(8,128)S(1)}, f32[264,128]{1,0:T(8,128)S(1)}, u32[]{:S(2)}, u32[]{:S(2)}) %collective-permute-start.5) | collective-permute-done | bytes 135200 | tf_op jit(solution)/shard_map/ppermute | solution.py:178
  53.9 0.0 collective-permute-done.6.refs_1_
  53.9 0.0 collective-permute-done.7.refs_2_
  53.9 5.2 %collective-permute-done.8.refs_3_ = f32[2,2,32,1024]{3,2,1,0:T(8,128)S(1)} collective-permute-done((f32[2,2,32,1024]{3,2,1,0:T(8,128)}, f32[2,2,32,1024]{3,2,1,0:T(8,128)S(1)}, u32[]{:S(2)}, u32[]{:S(2)}) %collective-permute-start.8) | collective-permute-done | bytes 524320 | tf_op jit(solution)/shard_map/ppermute | solution.py:368
  59.1 1.7 %shard_map.52 = (f32[2,256,1024]{2,1,0:T(8,128)S(1)}, f32[264,128]{1,0:T(8,128)S(1)}, f32[264,128]{1,0:T(8,128)S(1)}) custom-call(f32[1,1024]{1,0:T(1,128)S(1)} %bitcast.3, f32[2,2,32,1024]{3,2,1,0:T(8,128)S(1)} %get-tuple-element.40.refs_0_, f32[2,2,32,1024]{3,2,1,0:T(8,128)S(1)} %collective-permute-done.6.refs_1_, ...), custom_call_target="tpu_custom_call" | custom-call | flops 1000 | bytes 1000 | tf_op jit(solution)/shard_map/pallas_call | solution.py:148
  60.8 2.3 %collective-permute-start.9 = (f32[264,128]{1,0:T(8,128)S(1)}, f32[264,128]{1,0:T(8,128)S(1)}, u32[]{:S(2)}, u32[]{:S(2)}) collective-permute-start(f32[264,128]{1,0:T(8,128)S(1)} %get-tuple-element.45), channel_id=1, source_target_pairs={{0,1},{1,0},{2,3},{3,2},{4,5},{5,4},{6,7},{7,6},{8,9},{9,8},{10,11... | collective-permute-start | bytes 405512 | tf_op jit(solution)/shard_map/ppermute | solution.py:178
  63.0 1.2 %collective-permute-start.15 = (f32[264,128]{1,0:T(8,128)S(1)}, f32[264,128]{1,0:T(8,128)S(1)}, u32[]{:S(2)}, u32[]{:S(2)}) collective-permute-start(f32[264,128]{1,0:T(8,128)S(1)} %add.32), channel_id=1, source_target_pairs={{0,8},{1,3},{2,10},{3,1},{4,12},{5,7},{6,14},{7,5},{8,0},{9,11},{1... | collective-permute-start | bytes 405512 | tf_op jit(solution)/shard_map/ppermute | solution.py:178
  64.2 0.0 collective-permute-done.9
  64.3 1.4 %collective-permute-start.10 = (f32[264,128]{1,0:T(8,128)S(1)}, f32[264,128]{1,0:T(8,128)S(1)}, u32[]{:S(2)}, u32[]{:S(2)}) collective-permute-start(f32[264,128]{1,0:T(8,128)S(1)} %add.33), channel_id=1, source_target_pairs={{0,2},{1,9},{2,0},{3,11},{4,6},{5,13},{6,4},{7,15},{8,10},{9,1},{1... | collective-permute-start | bytes 405512 | tf_op jit(solution)/shard_map/ppermute | solution.py:178
  65.6 1.5 %collective-permute-done.15 = f32[264,128]{1,0:T(8,128)S(1)} collective-permute-done((f32[264,128]{1,0:T(8,128)S(1)}, f32[264,128]{1,0:T(8,128)S(1)}, u32[]{:S(2)}, u32[]{:S(2)}) %collective-permute-start.15) | collective-permute-done | bytes 135200 | tf_op jit(solution)/shard_map/ppermute | solution.py:178
  67.2 2.6 %collective-permute-start.16 = (f32[264,128]{1,0:T(8,128)S(1)}, f32[264,128]{1,0:T(8,128)S(1)}, u32[]{:S(2)}, u32[]{:S(2)}) collective-permute-start(f32[264,128]{1,0:T(8,128)S(1)} %add.38), channel_id=1, source_target_pairs={{0,24},{1,7},{2,26},{3,5},{4,28},{5,3},{6,30},{7,1},{8,16},{9,15},... | collective-permute-start | bytes 405512 | tf_op jit(solution)/shard_map/ppermute | solution.py:178
  69.8 0.0 collective-permute-done.10
  69.8 2.8 %collective-permute-start.11 = (f32[264,128]{1,0:T(8,128)S(1)}, f32[264,128]{1,0:T(8,128)S(1)}, u32[]{:S(2)}, u32[]{:S(2)}) collective-permute-start(f32[264,128]{1,0:T(8,128)S(1)} %add.34), channel_id=1, source_target_pairs={{0,6},{1,25},{2,4},{3,27},{4,2},{5,29},{6,0},{7,31},{8,14},{9,17},... | collective-permute-start | bytes 405512 | tf_op jit(solution)/shard_map/ppermute | solution.py:178
  72.6 0.0 collective-permute-done.16
  72.6 3.3 %collective-permute-done.11 = f32[264,128]{1,0:T(8,128)S(1)} collective-permute-done((f32[264,128]{1,0:T(8,128)S(1)}, f32[264,128]{1,0:T(8,128)S(1)}, u32[]{:S(2)}, u32[]{:S(2)}) %collective-permute-start.11) | collective-permute-done | bytes 135200 | tf_op jit(solution)/shard_map/ppermute | solution.py:178
  75.9 1.3 %collective-permute-start.12 = (f32[264,128]{1,0:T(8,128)S(1)}, f32[264,128]{1,0:T(8,128)S(1)}, u32[]{:S(2)}, u32[]{:S(2)}) collective-permute-start(f32[264,128]{1,0:T(8,128)S(1)} %add.35), channel_id=1, source_target_pairs={{0,8},{1,3},{2,10},{3,1},{4,12},{5,7},{6,14},{7,5},{8,0},{9,11},{1... | collective-permute-start | bytes 405512 | tf_op jit(solution)/shard_map/ppermute | solution.py:178
  77.3 4.3 %shard_map.54.in_ref = f32[256,512]{1,0:T(8,128)S(1)} custom-call(f32[264,128]{1,0:T(8,128)S(1)} %add.39.in_ref), custom_call_target="tpu_custom_call" | custom-call | flops 2147483648 | bytes 1000 | tf_op jit(solution)/shard_map/pallas_call | solution.py:279
  81.6 0.0 collective-permute-done.12
  81.6 1.9 %collective-permute-start.13 = (f32[264,128]{1,0:T(8,128)S(1)}, f32[264,128]{1,0:T(8,128)S(1)}, u32[]{:S(2)}, u32[]{:S(2)}) collective-permute-start(f32[264,128]{1,0:T(8,128)S(1)} %add.36), channel_id=1, source_target_pairs={{0,24},{1,7},{2,26},{3,5},{4,28},{5,3},{6,30},{7,1},{8,16},{9,15},... | collective-permute-start | bytes 405512 | tf_op jit(solution)/shard_map/ppermute | solution.py:178
  83.5 3.5 %shard_map.55.mine_ref = f32[2,256,256]{2,1,0:T(8,128)S(1)} custom-call(f32[256,512]{1,0:T(8,128)S(1)} %shard_map.54.in_ref), custom_call_target="tpu_custom_call" | custom-call | flops 2147483648 | bytes 1000 | tf_op jit(solution)/shard_map/pallas_call | solution.py:279
  87.0 1.5 %collective-permute-start.17 = (f32[2,256,256]{2,1,0:T(8,128)S(1)}, f32[2,256,256]{2,1,0:T(8,128)S(1)}, u32[]{:S(2)}, u32[]{:S(2)}) collective-permute-start(f32[2,256,256]{2,1,0:T(8,128)S(1)} %shard_map.55.mine_ref), channel_id=1, source_target_pairs={{0,1},{1,0},{2,3},{3,2},{4,5},{5,4},{6,7},{7,6},{8,9},{9,8},{10,11... | collective-permute-start | bytes 1572872 | tf_op jit(solution)/shard_map/ppermute | solution.py:178
  88.5 0.0 collective-permute-done.13
  88.5 7.8 %shard_map.53.mine_ref = f32[2,256,256]{2,1,0:T(8,128)S(1)} custom-call(f32[264,128]{1,0:T(8,128)S(1)} %add.37.in_ref), custom_call_target="tpu_custom_call" | custom-call | flops 4294967296 | bytes 1000 | tf_op jit(solution)/shard_map/pallas_call | solution.py:279
  96.3 1.5 %collective-permute-start.14 = (f32[2,256,256]{2,1,0:T(8,128)S(1)}, f32[2,256,256]{2,1,0:T(8,128)S(1)}, u32[]{:S(2)}, u32[]{:S(2)}) collective-permute-start(f32[2,256,256]{2,1,0:T(8,128)S(1)} %shard_map.53.mine_ref), channel_id=1, source_target_pairs={{0,1},{1,0},{2,3},{3,2},{4,5},{5,4},{6,7},{7,6},{8,9},{9,8},{10,11... | collective-permute-start | bytes 1572872 | tf_op jit(solution)/shard_map/ppermute | solution.py:178
  97.8 0.0 collective-permute-done.17.other_ref
  97.8 2.1 %shard_map.56 = (f32[4,1024,256]{2,1,0:T(8,128)}, f32[4,256,256]{2,1,0:T(8,128)}) custom-call(f32[2,256,256]{2,1,0:T(8,128)S(1)} %shard_map.55.mine_ref, f32[2,256,256]{2,1,0:T(8,128)S(1)} %collective-permute-done.17.other_ref, f32[2,256,1024]{2,1,0:T(8,128)S(1)} %get-tuple-element.49.mt_ref), custom_call_target="tpu_custom_call" | custom-call | flops 1000 | bytes 1000 | tf_op jit(solution)/shard_map/pallas_call | solution.py:333
  99.8 0.0 collective-permute-done.14.other_ref
  99.9 2.1 %shard_map.57 = (f32[4,1024,256]{2,1,0:T(8,128)}, f32[4,256,256]{2,1,0:T(8,128)}) custom-call(f32[2,256,256]{2,1,0:T(8,128)S(1)} %shard_map.53.mine_ref, f32[2,256,256]{2,1,0:T(8,128)S(1)} %collective-permute-done.14.other_ref, f32[2,256,1024]{2,1,0:T(8,128)S(1)} %get-tuple-element.47.mt_ref, ...), custom_call_target="tpu_custom_call", output_to_operand_aliasing={{0}: (3, {}), {1}: (4, {})} | custom-call | flops 1000 | bytes 1000 | tf_op jit(solution)/shard_map/pallas_call | solution.py:333
  (10 shorter events, 0.2 us)
Async XLA Ops:
  0.6 0.7 copy-start.1
  1.3 36.0 %copy-start = (f32[1024]{0:T(1024)S(1)}, f32[1024]{0:T(1024)}, u32[]{:S(2)}) copy-start(f32[1024]{0:T(1024)} %param.4) | copy-start | bytes 12292
  8.8 16.3 %collective-permute-start = (f32[2,2,32,1024]{3,2,1,0:T(8,128)S(1)}, f32[2,2,32,1024]{3,2,1,0:T(8,128)S(1)}, u32[]{:S(2)}, u32[]{:S(2)}) collective-permute-start(f32[2,2,32,1024]{3,2,1,0:T(8,128)S(1)} %get-tuple-element.29), channel_id=1, source_target_pairs={{0,32},{32,64},{64,96},{96,0},{1,33},{33,65},{65,97},{97,1},{2,34}... | collective-permute-start | bytes 1572872 | tf_op jit(solution)/shard_map/ppermute | solution.py:368
  11.3 13.8 %collective-permute-start.1 = (f32[2,2,32,1024]{3,2,1,0:T(8,128)S(1)}, f32[2,2,32,1024]{3,2,1,0:T(8,128)S(1)}, u32[]{:S(2)}, u32[]{:S(2)}) collective-permute-start(f32[2,2,32,1024]{3,2,1,0:T(8,128)S(1)} %get-tuple-element.32), channel_id=1, source_target_pairs={{0,96},{32,0},{64,32},{96,64},{1,97},{33,1},{65,33},{97,65},{2,98}... | collective-permute-start | bytes 1572872 | tf_op jit(solution)/shard_map/ppermute | solution.py:368
  13.5 23.7 %collective-permute-start.2 = (f32[2,2,32,1024]{3,2,1,0:T(8,128)S(1)}, f32[2,2,32,1024]{3,2,1,0:T(8,128)S(1)}, u32[]{:S(2)}, u32[]{:S(2)}) collective-permute-start(f32[2,2,32,1024]{3,2,1,0:T(8,128)S(1)} %get-tuple-element.35), channel_id=1, source_target_pairs={{0,64},{32,96},{64,0},{96,32},{1,65},{33,97},{65,1},{97,33},{2,66}... | collective-permute-start | bytes 1572872 | tf_op jit(solution)/shard_map/ppermute | solution.py:368
  25.1 28.7 %collective-permute-start.6 = (f32[2,2,32,1024]{3,2,1,0:T(8,128)S(1)}, f32[2,2,32,1024]{3,2,1,0:T(8,128)S(1)}, u32[]{:S(2)}, u32[]{:S(2)}) collective-permute-start(f32[2,2,32,1024]{3,2,1,0:T(8,128)S(1)} %get-tuple-element.41), channel_id=1, source_target_pairs={{0,32},{32,64},{64,96},{96,0},{1,33},{33,65},{65,97},{97,1},{2,34}... | collective-permute-start | bytes 1572872 | tf_op jit(solution)/shard_map/ppermute | solution.py:368
  25.1 28.8 %collective-permute-start.7 = (f32[2,2,32,1024]{3,2,1,0:T(8,128)S(1)}, f32[2,2,32,1024]{3,2,1,0:T(8,128)S(1)}, u32[]{:S(2)}, u32[]{:S(2)}) collective-permute-start(f32[2,2,32,1024]{3,2,1,0:T(8,128)S(1)} %get-tuple-element.42), channel_id=1, source_target_pairs={{0,96},{32,0},{64,32},{96,64},{1,97},{33,1},{65,33},{97,65},{2,98}... | collective-permute-start | bytes 1572872 | tf_op jit(solution)/shard_map/ppermute | solution.py:368
  37.2 21.8 %collective-permute-start.8 = (f32[2,2,32,1024]{3,2,1,0:T(8,128)}, f32[2,2,32,1024]{3,2,1,0:T(8,128)S(1)}, u32[]{:S(2)}, u32[]{:S(2)}) collective-permute-start(f32[2,2,32,1024]{3,2,1,0:T(8,128)} %get-tuple-element.43), channel_id=1, source_target_pairs={{0,64},{32,96},{64,0},{96,32},{1,65},{33,97},{65,1},{97,33},{2,66}... | collective-permute-start | bytes 1572872 | tf_op jit(solution)/shard_map/ppermute | solution.py:368
  38.9 5.1 %collective-permute-start.3 = (f32[264,128]{1,0:T(8,128)S(1)}, f32[264,128]{1,0:T(8,128)S(1)}, u32[]{:S(2)}, u32[]{:S(2)}) collective-permute-start(f32[264,128]{1,0:T(8,128)S(1)} %get-tuple-element.38), channel_id=1, source_target_pairs={{0,1},{1,0},{2,3},{3,2},{4,5},{5,4},{6,7},{7,6},{8,9},{9,8},{10,11... | collective-permute-start | bytes 405512 | tf_op jit(solution)/shard_map/ppermute | solution.py:178
  44.1 4.2 %collective-permute-start.4 = (f32[264,128]{1,0:T(8,128)S(1)}, f32[264,128]{1,0:T(8,128)S(1)}, u32[]{:S(2)}, u32[]{:S(2)}) collective-permute-start(f32[264,128]{1,0:T(8,128)S(1)} %add.30), channel_id=1, source_target_pairs={{0,2},{1,9},{2,0},{3,11},{4,6},{5,13},{6,4},{7,15},{8,10},{9,1},{1... | collective-permute-start | bytes 405512 | tf_op jit(solution)/shard_map/ppermute | solution.py:178
  48.3 5.5 %collective-permute-start.5 = (f32[264,128]{1,0:T(8,128)S(1)}, f32[264,128]{1,0:T(8,128)S(1)}, u32[]{:S(2)}, u32[]{:S(2)}) collective-permute-start(f32[264,128]{1,0:T(8,128)S(1)} %add.31), channel_id=1, source_target_pairs={{0,6},{1,25},{2,4},{3,27},{4,2},{5,29},{6,0},{7,31},{8,14},{9,17},... | collective-permute-start | bytes 405512 | tf_op jit(solution)/shard_map/ppermute | solution.py:178
  60.8 3.5 %collective-permute-start.9 = (f32[264,128]{1,0:T(8,128)S(1)}, f32[264,128]{1,0:T(8,128)S(1)}, u32[]{:S(2)}, u32[]{:S(2)}) collective-permute-start(f32[264,128]{1,0:T(8,128)S(1)} %get-tuple-element.45), channel_id=1, source_target_pairs={{0,1},{1,0},{2,3},{3,2},{4,5},{5,4},{6,7},{7,6},{8,9},{9,8},{10,11... | collective-permute-start | bytes 405512 | tf_op jit(solution)/shard_map/ppermute | solution.py:178
  63.0 4.2 %collective-permute-start.15 = (f32[264,128]{1,0:T(8,128)S(1)}, f32[264,128]{1,0:T(8,128)S(1)}, u32[]{:S(2)}, u32[]{:S(2)}) collective-permute-start(f32[264,128]{1,0:T(8,128)S(1)} %add.32), channel_id=1, source_target_pairs={{0,8},{1,3},{2,10},{3,1},{4,12},{5,7},{6,14},{7,5},{8,0},{9,11},{1... | collective-permute-start | bytes 405512 | tf_op jit(solution)/shard_map/ppermute | solution.py:178
  64.3 5.5 %collective-permute-start.10 = (f32[264,128]{1,0:T(8,128)S(1)}, f32[264,128]{1,0:T(8,128)S(1)}, u32[]{:S(2)}, u32[]{:S(2)}) collective-permute-start(f32[264,128]{1,0:T(8,128)S(1)} %add.33), channel_id=1, source_target_pairs={{0,2},{1,9},{2,0},{3,11},{4,6},{5,13},{6,4},{7,15},{8,10},{9,1},{1... | collective-permute-start | bytes 405512 | tf_op jit(solution)/shard_map/ppermute | solution.py:178
  67.2 5.4 %collective-permute-start.16 = (f32[264,128]{1,0:T(8,128)S(1)}, f32[264,128]{1,0:T(8,128)S(1)}, u32[]{:S(2)}, u32[]{:S(2)}) collective-permute-start(f32[264,128]{1,0:T(8,128)S(1)} %add.38), channel_id=1, source_target_pairs={{0,24},{1,7},{2,26},{3,5},{4,28},{5,3},{6,30},{7,1},{8,16},{9,15},... | collective-permute-start | bytes 405512 | tf_op jit(solution)/shard_map/ppermute | solution.py:178
  69.8 6.1 %collective-permute-start.11 = (f32[264,128]{1,0:T(8,128)S(1)}, f32[264,128]{1,0:T(8,128)S(1)}, u32[]{:S(2)}, u32[]{:S(2)}) collective-permute-start(f32[264,128]{1,0:T(8,128)S(1)} %add.34), channel_id=1, source_target_pairs={{0,6},{1,25},{2,4},{3,27},{4,2},{5,29},{6,0},{7,31},{8,14},{9,17},... | collective-permute-start | bytes 405512 | tf_op jit(solution)/shard_map/ppermute | solution.py:178
  75.9 5.6 %collective-permute-start.12 = (f32[264,128]{1,0:T(8,128)S(1)}, f32[264,128]{1,0:T(8,128)S(1)}, u32[]{:S(2)}, u32[]{:S(2)}) collective-permute-start(f32[264,128]{1,0:T(8,128)S(1)} %add.35), channel_id=1, source_target_pairs={{0,8},{1,3},{2,10},{3,1},{4,12},{5,7},{6,14},{7,5},{8,0},{9,11},{1... | collective-permute-start | bytes 405512 | tf_op jit(solution)/shard_map/ppermute | solution.py:178
  81.6 6.9 %collective-permute-start.13 = (f32[264,128]{1,0:T(8,128)S(1)}, f32[264,128]{1,0:T(8,128)S(1)}, u32[]{:S(2)}, u32[]{:S(2)}) collective-permute-start(f32[264,128]{1,0:T(8,128)S(1)} %add.36), channel_id=1, source_target_pairs={{0,24},{1,7},{2,26},{3,5},{4,28},{5,3},{6,30},{7,1},{8,16},{9,15},... | collective-permute-start | bytes 405512 | tf_op jit(solution)/shard_map/ppermute | solution.py:178
  87.0 10.7 %collective-permute-start.17 = (f32[2,256,256]{2,1,0:T(8,128)S(1)}, f32[2,256,256]{2,1,0:T(8,128)S(1)}, u32[]{:S(2)}, u32[]{:S(2)}) collective-permute-start(f32[2,256,256]{2,1,0:T(8,128)S(1)} %shard_map.55.mine_ref), channel_id=1, source_target_pairs={{0,1},{1,0},{2,3},{3,2},{4,5},{5,4},{6,7},{7,6},{8,9},{9,8},{10,11... | collective-permute-start | bytes 1572872 | tf_op jit(solution)/shard_map/ppermute | solution.py:178
  96.3 3.6 %collective-permute-start.14 = (f32[2,256,256]{2,1,0:T(8,128)S(1)}, f32[2,256,256]{2,1,0:T(8,128)S(1)}, u32[]{:S(2)}, u32[]{:S(2)}) collective-permute-start(f32[2,256,256]{2,1,0:T(8,128)S(1)} %shard_map.53.mine_ref), channel_id=1, source_target_pairs={{0,1},{1,0},{2,3},{3,2},{4,5},{5,4},{6,7},{7,6},{8,9},{9,8},{10,11... | collective-permute-start | bytes 1572872 | tf_op jit(solution)/shard_map/ppermute | solution.py:178

commit v3 on v2

--- a/solution.py
+++ b/solution.py
@@ -9,12 +9,11 @@
 from jax.sharding import PartitionSpec as P
 
 HIGHEST = lax.Precision.HIGHEST
-HOPS = (0, 1, 3, 2)
+HOPS = (0, 2, 1, 3)
 GROUPS = ((0, 1), (2, 3))
 PANEL = 32
+PAIRS = ((0, 0), (0, 1), (1, 0), (0, 2), (2, 0), (1, 1))
 CUTS = (4,)
-STEPS = (0, 1, 2, 3)
-EARLY = 2
 IN_VMEM = pl.BlockSpec(memory_space=pltpu.VMEM)
 IN_HBM = pl.BlockSpec(memory_space=pltpu.HBM)
 SMALL = pl.CostEstimate(flops=1000, bytes_accessed=1000, transcendentals=0)
@@ -228,14 +227,33 @@
             for t in tiles:
                 work[base + 8 * i : base + 8 * i + 8, 128 * t : 128 * t + 128] = done[i][t]
         after = base + PANEL
-        first = after // 128
-        for blk in range(first, half):
-            lo, hi = max(after, 128 * blk), 128 * blk + 128
-            left = work[base:after, 128 * blk : hi]
-            for c0, c1 in ((128 * first, n), (n, n + (after + 127) // 128 * 128)):
-                right = work[base:after, c0:c1]
-                update = dot(left, right, ((0,), (0,)), HIGHEST)
-                work[lo:hi, c0:c1] = work[lo:hi, c0:c1] - update[lo - 128 * blk :, :]
+        if after < n:
+            first = after // 128
+            spans = ((128 * first, n), (n, n + (after + 127) // 128 * 128))
+            right = [stacked(work[base:after, c0:c1], 1) for c0, c1 in spans]
+            ends = [after + PANEL, n] if after + PANEL < n else [n]
+            left = {
+                blk: stacked(work[base:after, 128 * blk : 128 * blk + 128], 0)
+                for blk in range(first, half)
+            }
+            for r0, r1 in zip([after] + ends, ends):
+                for blk in range(r0 // 128, (r1 + 127) // 128):
+                    lo, hi = max(r0, 128 * blk), min(r1, 128 * blk + 128)
+                    part = left[blk][lo - 128 * blk : hi - 128 * blk, :]
+                    for (c0, c1), other in zip(spans, right):
+                        work[lo:hi, c0:c1] = work[lo:hi, c0:c1] - dot(part, other, ((1,), (0,)))
+
+
+def stacked(value, side):
+    parts = []
+    for _ in range(3):
+        parts.append(value.astype(jnp.bfloat16).astype(jnp.float32))
+        value = value - parts[-1]
+    chosen = [parts[pair[side]] for pair in PAIRS]
+    both = jnp.concatenate(chosen, axis=0)
+    if side == 0:
+        both = both.T
+    return both.astype(jnp.bfloat16)
 
 
 def load_gram(work, packed):
@@ -367,15 +385,15 @@
                 piece, arrived[-1][h] = lax.optimization_barrier((piece, arrived[-1][h]))
             got.append(lax.ppermute(piece, "freq", [(i, (i + hop) % n_freq) for i in range(n_freq)]))
         arrived.append(got)
-    sums = []
-    for got in arrived:
-        mt, mine, other = gram(volumes, got)
-        value = add_steps(mine + swap(other, "core"), STEPS[:EARLY])
-        value, volumes = lax.optimization_barrier((value, volumes))
-        sums.append((mt, value))
+    mt_first, mine, other = gram(volumes, arrived[0])
+    first = add_steps(mine + swap(other, "core"), (0, 1))
+    first, volumes = lax.optimization_barrier((first, volumes))
+    mt_second, mine, other = gram(volumes, arrived[1])
+    both = add_steps(jnp.stack([first, mine + swap(other, "core")]), (2, 3))
+    second = add_steps(both[1], (0, 1))
     outs = ()
-    for js, (mt, value) in zip(GROUPS, sums):
-        value = factor_call(add_steps(value, STEPS[EARLY:]), CUTS if js[0] == 0 else ())
+    for js, mt, value, cuts in ((GROUPS[0], mt_first, both[0], CUTS), (GROUPS[1], mt_second, second, ())):
+        value = factor_call(value, cuts)
         outs = modes_call(js, n_local, root_rows, value, swap(value, "core"), mt, outs)
     return tuple(outs)
 

time: 102 us -> 101 us (level)
  waiting for transfers between devices: 35.7 us -> 40.2 us
  starting transfers between devices: 34.1 us -> 30.6 us
  Pallas kernels: 30.6 us -> 28.6 us
    ppermute x12 -> x10, starting transfers between devices: 24.7 us -> 17.3 us  [swap(): return lax.ppermute(value, 'space', space_pairs(kind))]
    ppermute x12 -> x10, waiting for transfers between devices: 11.4 us -> 16.3 us  [swap(): return lax.ppermute(value, 'space', space_pairs(kind))]
    ppermute x6, starting transfers between devices: 9.34 us -> 13.3 us  [on_device(): lax.ppermute(piece, 'freq', [(i, (i + hop) % n_freq) for i in range(n_fre...]
    pallas_call x3, Pallas kernels: 15.6 us -> 13.6 us  [factor_call(): pl.pallas_call(functools.partial(factor_kernel, begin, end), out_shape=ja...]
  transfers between devices with their start and end apart: 18 -> 16, of which waited for: 8 -> 9; matrix products, arithmetic and copies ran while one was open for 0% -> 0% of each run, Pallas kernels for 19% -> 17%
where the time goes in v3:
time: 101 us
  waiting for transfers between devices  40.2 us (40%)
  starting transfers between devices  30.6 us (30%)
  Pallas kernels  28.6 us (28%)
    ppermute x6, waiting for transfers between devices, on_device(): lax.ppermute(piece, 'freq', [(i, (i + hop) % n_freq) for i in range(n_fre...  23.9 us
    ppermute x10, starting transfers between devices, swap(): return lax.ppermute(value, 'space', space_pairs(kind))  17.3 us
    ppermute x10, waiting for transfers between devices, swap(): return lax.ppermute(value, 'space', space_pairs(kind))  16.3 us
    pallas_call x3, Pallas kernels, factor_call(): pl.pallas_call(functools.partial(factor_kernel, begin, end), out_shape=ja...  13.6 us
    ppermute x6, starting transfers between devices, on_device(): lax.ppermute(piece, 'freq', [(i, (i + hop) % n_freq) for i in range(n_fre...  13.3 us
    pallas_call x1, Pallas kernels, transform(): pl.pallas_call(transform_kernel, out_shape=shapes, in_specs=[IN_HBM, IN_H...  7.51 us
    pallas_call x2, Pallas kernels, modes_call(): pl.pallas_call(functools.partial(modes_kernel, js, root_rows), out_shape=...  4.15 us
    pallas_call x2, Pallas kernels, gram(): pl.pallas_call(gram_kernel, out_shape=[jax.ShapeDtypeStruct((nj, n, n_x),...  3.35 us
  transfers between devices with their start and end apart: 16, of which 9 were waited for; matrix products, arithmetic and copies ran while one was open for 0% of the time, Pallas kernels for 17%

profile of v3, /device:TPU:1, one launch (start us, length us, event | category | flops | bytes accessed | tf_op | source)
XLA Modules:
  0.0 101.2 jit_solution(14020020597531319885)
XLA Ops:
  0.6 0.0 copy-start.1
  0.6 0.6 copy-done.1
  1.3 0.0 copy-start
  1.3 7.5 %shard_map.50 = (f32[2,2,32,1024]{3,2,1,0:T(8,128)S(1)}, f32[2,2,32,1024]{3,2,1,0:T(8,128)S(1)}, f32[2,2,32,1024]{3,2,1,0:T(8,128)S(1)}, f32[2,2,32,1024]{3,2,1,...) custom-call(s32[16]{0:T(128)S(1)} %copy-done.1, ...), custom_call_target="tpu_custom_call" | custom-call | flops 1000 | bytes 1000 | tf_op jit(solution)/shard_map/pallas_call | solution.py:99
  8.8 4.5 %collective-permute-start = (f32[2,2,32,1024]{3,2,1,0:T(8,128)S(1)}, f32[2,2,32,1024]{3,2,1,0:T(8,128)S(1)}, u32[]{:S(2)}, u32[]{:S(2)}) collective-permute-start(f32[2,2,32,1024]{3,2,1,0:T(8,128)S(1)} %get-tuple-element.28), channel_id=1, source_target_pairs={{0,64},{32,96},{64,0},{96,32},{1,65},{33,97},{65,1},{97,33},{2,66}... | collective-permute-start | bytes 1572872 | tf_op jit(solution)/shard_map/ppermute | solution.py:386
  13.3 0.7 collective-permute-start.1
  14.1 1.9 %collective-permute-start.2 = (f32[2,2,32,1024]{3,2,1,0:T(8,128)S(1)}, f32[2,2,32,1024]{3,2,1,0:T(8,128)S(1)}, u32[]{:S(2)}, u32[]{:S(2)}) collective-permute-start(f32[2,2,32,1024]{3,2,1,0:T(8,128)S(1)} %get-tuple-element.34), channel_id=1, source_target_pairs={{0,96},{32,0},{64,32},{96,64},{1,97},{33,1},{65,33},{97,65},{2,98}... | collective-permute-start | bytes 1572872 | tf_op jit(solution)/shard_map/ppermute | solution.py:386
  16.0 9.0 %collective-permute-done.refs_1_ = f32[2,2,32,1024]{3,2,1,0:T(8,128)S(1)} collective-permute-done((f32[2,2,32,1024]{3,2,1,0:T(8,128)S(1)}, f32[2,2,32,1024]{3,2,1,0:T(8,128)S(1)}, u32[]{:S(2)}, u32[]{:S(2)}) %collective-permute-start) | collective-permute-done | bytes 524320 | tf_op jit(solution)/shard_map/ppermute | solution.py:386
  25.0 2.7 %collective-permute-start.6 = (f32[2,2,32,1024]{3,2,1,0:T(8,128)S(1)}, f32[2,2,32,1024]{3,2,1,0:T(8,128)S(1)}, u32[]{:S(2)}, u32[]{:S(2)}) collective-permute-start(f32[2,2,32,1024]{3,2,1,0:T(8,128)S(1)} %get-tuple-element.41), channel_id=1, source_target_pairs={{0,64},{32,96},{64,0},{96,32},{1,65},{33,97},{65,1},{97,33},{2,66}... | collective-permute-start | bytes 1572872 | tf_op jit(solution)/shard_map/ppermute | solution.py:386
  27.7 9.9 %collective-permute-done.1.refs_2_ = f32[2,2,32,1024]{3,2,1,0:T(8,128)S(1)} collective-permute-done((f32[2,2,32,1024]{3,2,1,0:T(8,128)S(1)}, f32[2,2,32,1024]{3,2,1,0:T(8,128)S(1)}, u32[]{:S(2)}, u32[]{:S(2)}) %collective-permute-start.1) | collective-permute-done | bytes 524320 | tf_op jit(solution)/shard_map/ppermute | solution.py:386
  37.6 0.0 collective-permute-start.7
  37.6 0.0 collective-permute-done.2.refs_3_
  37.6 3.4 %collective-permute-start.8 = (f32[2,2,32,1024]{3,2,1,0:T(8,128)}, f32[2,2,32,1024]{3,2,1,0:T(8,128)S(1)}, u32[]{:S(2)}, u32[]{:S(2)}) collective-permute-start(f32[2,2,32,1024]{3,2,1,0:T(8,128)} %get-tuple-element.43), channel_id=1, source_target_pairs={{0,96},{32,0},{64,32},{96,64},{1,97},{33,1},{65,33},{97,65},{2,98}... | collective-permute-start | bytes 1572872 | tf_op jit(solution)/shard_map/ppermute | solution.py:386
  41.1 0.0 copy-done
  41.1 1.7 %shard_map.51 = (f32[2,256,1024]{2,1,0:T(8,128)S(1)}, f32[264,128]{1,0:T(8,128)S(1)}, f32[264,128]{1,0:T(8,128)S(1)}) custom-call(f32[1,1024]{1,0:T(1,128)S(1)} %bitcast.11, f32[2,2,32,1024]{3,2,1,0:T(8,128)S(1)} %get-tuple-element.26.refs_0_, f32[2,2,32,1024]{3,2,1,0:T(8,128)S(1)} %collective-permute-done.refs_1_, ...), custom_call_target="tpu_custom_call" | custom-call | flops 1000 | bytes 1000 | tf_op jit(solution)/shard_map/pallas_call | solution.py:147
  42.7 0.9 collective-permute-start.3
  43.7 1.0 collective-permute-done.3
  44.7 1.4 %collective-permute-start.4 = (f32[264,128]{1,0:T(8,128)S(1)}, f32[264,128]{1,0:T(8,128)S(1)}, u32[]{:S(2)}, u32[]{:S(2)}) collective-permute-start(f32[264,128]{1,0:T(8,128)S(1)} %add.24), channel_id=1, source_target_pairs={{0,2},{1,9},{2,0},{3,11},{4,6},{5,13},{6,4},{7,15},{8,10},{9,1},{1... | collective-permute-start | bytes 405512 | tf_op jit(solution)/shard_map/ppermute | solution.py:177
  46.1 2.9 %collective-permute-done.4 = f32[264,128]{1,0:T(8,128)S(1)} collective-permute-done((f32[264,128]{1,0:T(8,128)S(1)}, f32[264,128]{1,0:T(8,128)S(1)}, u32[]{:S(2)}, u32[]{:S(2)}) %collective-permute-start.4) | collective-permute-done | bytes 135200 | tf_op jit(solution)/shard_map/ppermute | solution.py:177
  49.0 2.8 %collective-permute-start.5 = (f32[264,128]{1,0:T(8,128)S(1)}, f32[264,128]{1,0:T(8,128)S(1)}, u32[]{:S(2)}, u32[]{:S(2)}) collective-permute-start(f32[264,128]{1,0:T(8,128)S(1)} %add.25), channel_id=1, source_target_pairs={{0,6},{1,25},{2,4},{3,27},{4,2},{5,29},{6,0},{7,31},{8,14},{9,17},... | collective-permute-start | bytes 405512 | tf_op jit(solution)/shard_map/ppermute | solution.py:177
  51.8 2.7 %collective-permute-done.5 = f32[264,128]{1,0:T(8,128)S(1)} collective-permute-done((f32[264,128]{1,0:T(8,128)S(1)}, f32[264,128]{1,0:T(8,128)S(1)}, u32[]{:S(2)}, u32[]{:S(2)}) %collective-permute-start.5) | collective-permute-done | bytes 135200 | tf_op jit(solution)/shard_map/ppermute | solution.py:177
  54.5 0.0 collective-permute-done.6.refs_1_
  54.5 4.9 %collective-permute-done.7.refs_2_ = f32[2,2,32,1024]{3,2,1,0:T(8,128)S(1)} collective-permute-done((f32[2,2,32,1024]{3,2,1,0:T(8,128)S(1)}, f32[2,2,32,1024]{3,2,1,0:T(8,128)S(1)}, u32[]{:S(2)}, u32[]{:S(2)}) %collective-permute-start.7) | collective-permute-done | bytes 524320 | tf_op jit(solution)/shard_map/ppermute | solution.py:386
  59.4 0.0 collective-permute-done.8.refs_3_
  59.5 1.7 %shard_map.52 = (f32[2,256,1024]{2,1,0:T(8,128)S(1)}, f32[264,128]{1,0:T(8,128)S(1)}, f32[264,128]{1,0:T(8,128)S(1)}) custom-call(f32[1,1024]{1,0:T(1,128)S(1)} %bitcast.12, f32[2,2,32,1024]{3,2,1,0:T(8,128)S(1)} %get-tuple-element.40.refs_0_, f32[2,2,32,1024]{3,2,1,0:T(8,128)S(1)} %collective-permute-done.6.refs_1_, ...), custom_call_target="tpu_custom_call" | custom-call | flops 1000 | bytes 1000 | tf_op jit(solution)/shard_map/pallas_call | solution.py:147
  61.1 1.3 %collective-permute-start.9 = (f32[264,128]{1,0:T(8,128)S(1)}, f32[264,128]{1,0:T(8,128)S(1)}, u32[]{:S(2)}, u32[]{:S(2)}) collective-permute-start(f32[264,128]{1,0:T(8,128)S(1)} %get-tuple-element.45), channel_id=1, source_target_pairs={{0,1},{1,0},{2,3},{3,2},{4,5},{5,4},{6,7},{7,6},{8,9},{9,8},{10,11... | collective-permute-start | bytes 405512 | tf_op jit(solution)/shard_map/ppermute | solution.py:177
  62.5 1.0 collective-permute-done.9
  63.5 1.3 %collective-permute-start.10 = (f32[2,264,128]{2,1,0:T(8,128)S(1)}, f32[2,264,128]{2,1,0:T(8,128)S(1)}, u32[]{:S(2)}, u32[]{:S(2)}) collective-permute-start(f32[2,264,128]{2,1,0:T(8,128)S(1)} %pad_maximum_fusion), channel_id=1, source_target_pairs={{0,8},{1,3},{2,10},{3,1},{4,12},{5,7},{6,14},{7,5},{8,0},{9,11},{1... | collective-permute-start | bytes 811016 | tf_op jit(solution)/shard_map/ppermute | solution.py:177
  64.8 4.4 %collective-permute-done.10 = f32[2,264,128]{2,1,0:T(8,128)S(1)} collective-permute-done((f32[2,264,128]{2,1,0:T(8,128)S(1)}, f32[2,264,128]{2,1,0:T(8,128)S(1)}, u32[]{:S(2)}, u32[]{:S(2)}) %collective-permute-start.10) | collective-permute-done | bytes 270368 | tf_op jit(solution)/shard_map/ppermute | solution.py:177
  69.2 0.1 fusion.1
  69.2 2.6 %collective-permute-start.11 = (f32[2,264,128]{2,1,0:T(8,128)S(1)}, f32[2,264,128]{2,1,0:T(8,128)S(1)}, u32[]{:S(2)}, u32[]{:S(2)}) collective-permute-start(f32[2,264,128]{2,1,0:T(8,128)S(1)} %fusion.1), channel_id=1, source_target_pairs={{0,24},{1,7},{2,26},{3,5},{4,28},{5,3},{6,30},{7,1},{8,16},{9,15},... | collective-permute-start | bytes 811016 | tf_op jit(solution)/shard_map/ppermute | solution.py:177
  71.8 4.3 %collective-permute-done.11 = f32[2,264,128]{2,1,0:T(8,128)S(1)} collective-permute-done((f32[2,264,128]{2,1,0:T(8,128)S(1)}, f32[2,264,128]{2,1,0:T(8,128)S(1)}, u32[]{:S(2)}, u32[]{:S(2)}) %collective-permute-start.11) | collective-permute-done | bytes 270368 | tf_op jit(solution)/shard_map/ppermute | solution.py:177
  76.1 0.1 fusion.2
  76.2 1.1 %collective-permute-start.12 = (f32[264,128]{1,0:T(8,128)S(1)}, f32[264,128]{1,0:T(8,128)S(1)}, u32[]{:S(2)}, u32[]{:S(2)}) collective-permute-start(f32[264,128]{1,0:T(8,128)S(1)} %get-tuple-element.51), channel_id=1, source_target_pairs={{0,2},{1,9},{2,0},{3,11},{4,6},{5,13},{6,4},{7,15},{8,10},{9,1},{1... | collective-permute-start | bytes 405512 | tf_op jit(solution)/shard_map/ppermute | solution.py:177
  77.3 3.6 %shard_map.54.in_ref = f32[256,512]{1,0:T(8,128)S(1)} custom-call(f32[264,128]{1,0:T(8,128)S(1)} %get-tuple-element.50.in_ref), custom_call_target="tpu_custom_call" | custom-call | flops 2147483648 | bytes 1000 | tf_op jit(solution)/shard_map/pallas_call | solution.py:297
  80.9 0.0 collective-permute-done.12
  81.0 2.2 %collective-permute-start.13 = (f32[264,128]{1,0:T(8,128)S(1)}, f32[264,128]{1,0:T(8,128)S(1)}, u32[]{:S(2)}, u32[]{:S(2)}) collective-permute-start(f32[264,128]{1,0:T(8,128)S(1)} %fusion), channel_id=1, source_target_pairs={{0,6},{1,25},{2,4},{3,27},{4,2},{5,29},{6,0},{7,31},{8,14},{9,17},... | collective-permute-start | bytes 405512 | tf_op jit(solution)/shard_map/ppermute | solution.py:177
  83.2 3.2 %shard_map.55.mine_ref = f32[2,256,256]{2,1,0:T(8,128)S(1)} custom-call(f32[256,512]{1,0:T(8,128)S(1)} %shard_map.54.in_ref), custom_call_target="tpu_custom_call" | custom-call | flops 2147483648 | bytes 1000 | tf_op jit(solution)/shard_map/pallas_call | solution.py:297
  86.4 3.3 %collective-permute-start.15 = (f32[2,256,256]{2,1,0:T(8,128)S(1)}, f32[2,256,256]{2,1,0:T(8,128)S(1)}, u32[]{:S(2)}, u32[]{:S(2)}) collective-permute-start(f32[2,256,256]{2,1,0:T(8,128)S(1)} %shard_map.55.mine_ref), channel_id=1, source_target_pairs={{0,1},{1,0},{2,3},{3,2},{4,5},{5,4},{6,7},{7,6},{8,9},{9,8},{10,11... | collective-permute-start | bytes 1572872 | tf_op jit(solution)/shard_map/ppermute | solution.py:177
  89.7 0.0 collective-permute-done.13
  89.8 6.8 %shard_map.53.mine_ref = f32[2,256,256]{2,1,0:T(8,128)S(1)} custom-call(f32[264,128]{1,0:T(8,128)S(1)} %add.31.in_ref), custom_call_target="tpu_custom_call" | custom-call | flops 4294967296 | bytes 1000 | tf_op jit(solution)/shard_map/pallas_call | solution.py:297
  96.5 0.3 collective-permute-start.14
  96.9 0.0 collective-permute-done.15.other_ref
  96.9 2.1 %shard_map.56 = (f32[4,1024,256]{2,1,0:T(8,128)}, f32[4,256,256]{2,1,0:T(8,128)}) custom-call(f32[2,256,256]{2,1,0:T(8,128)S(1)} %shard_map.55.mine_ref, f32[2,256,256]{2,1,0:T(8,128)S(1)} %collective-permute-done.15.other_ref, f32[2,256,1024]{2,1,0:T(8,128)S(1)} %get-tuple-element.47.mt_ref), custom_call_target="tpu_custom_call" | custom-call | flops 1000 | bytes 1000 | tf_op jit(solution)/shard_map/pallas_call | solution.py:351
  99.0 0.0 collective-permute-done.14.other_ref
  99.0 2.1 %shard_map.57 = (f32[4,1024,256]{2,1,0:T(8,128)}, f32[4,256,256]{2,1,0:T(8,128)}) custom-call(f32[2,256,256]{2,1,0:T(8,128)S(1)} %shard_map.53.mine_ref, f32[2,256,256]{2,1,0:T(8,128)S(1)} %collective-permute-done.14.other_ref, f32[2,256,1024]{2,1,0:T(8,128)S(1)} %get-tuple-element.46.mt_ref, ...), custom_call_target="tpu_custom_call", output_to_operand_aliasing={{0}: (3, {}), {1}: (4, {})} | custom-call | flops 1000 | bytes 1000 | tf_op jit(solution)/shard_map/pallas_call | solution.py:351
  (8 shorter events, 0.2 us)
Async XLA Ops:
  0.6 0.7 copy-start.1
  1.3 39.8 %copy-start = (f32[1024]{0:T(1024)S(1)}, f32[1024]{0:T(1024)}, u32[]{:S(2)}) copy-start(f32[1024]{0:T(1024)} %param.4) | copy-start | bytes 12292
  8.8 16.2 %collective-permute-start = (f32[2,2,32,1024]{3,2,1,0:T(8,128)S(1)}, f32[2,2,32,1024]{3,2,1,0:T(8,128)S(1)}, u32[]{:S(2)}, u32[]{:S(2)}) collective-permute-start(f32[2,2,32,1024]{3,2,1,0:T(8,128)S(1)} %get-tuple-element.28), channel_id=1, source_target_pairs={{0,64},{32,96},{64,0},{96,32},{1,65},{33,97},{65,1},{97,33},{2,66}... | collective-permute-start | bytes 1572872 | tf_op jit(solution)/shard_map/ppermute | solution.py:386
  13.3 24.3 %collective-permute-start.1 = (f32[2,2,32,1024]{3,2,1,0:T(8,128)S(1)}, f32[2,2,32,1024]{3,2,1,0:T(8,128)S(1)}, u32[]{:S(2)}, u32[]{:S(2)}) collective-permute-start(f32[2,2,32,1024]{3,2,1,0:T(8,128)S(1)} %get-tuple-element.31), channel_id=1, source_target_pairs={{0,32},{32,64},{64,96},{96,0},{1,33},{33,65},{65,97},{97,1},{2,34}... | collective-permute-start | bytes 1572872 | tf_op jit(solution)/shard_map/ppermute | solution.py:386
  14.1 23.6 %collective-permute-start.2 = (f32[2,2,32,1024]{3,2,1,0:T(8,128)S(1)}, f32[2,2,32,1024]{3,2,1,0:T(8,128)S(1)}, u32[]{:S(2)}, u32[]{:S(2)}) collective-permute-start(f32[2,2,32,1024]{3,2,1,0:T(8,128)S(1)} %get-tuple-element.34), channel_id=1, source_target_pairs={{0,96},{32,0},{64,32},{96,64},{1,97},{33,1},{65,33},{97,65},{2,98}... | collective-permute-start | bytes 1572872 | tf_op jit(solution)/shard_map/ppermute | solution.py:386
  25.0 29.5 %collective-permute-start.6 = (f32[2,2,32,1024]{3,2,1,0:T(8,128)S(1)}, f32[2,2,32,1024]{3,2,1,0:T(8,128)S(1)}, u32[]{:S(2)}, u32[]{:S(2)}) collective-permute-start(f32[2,2,32,1024]{3,2,1,0:T(8,128)S(1)} %get-tuple-element.41), channel_id=1, source_target_pairs={{0,64},{32,96},{64,0},{96,32},{1,65},{33,97},{65,1},{97,33},{2,66}... | collective-permute-start | bytes 1572872 | tf_op jit(solution)/shard_map/ppermute | solution.py:386
  37.6 21.8 %collective-permute-start.7 = (f32[2,2,32,1024]{3,2,1,0:T(8,128)S(1)}, f32[2,2,32,1024]{3,2,1,0:T(8,128)S(1)}, u32[]{:S(2)}, u32[]{:S(2)}) collective-permute-start(f32[2,2,32,1024]{3,2,1,0:T(8,128)S(1)} %get-tuple-element.42), channel_id=1, source_target_pairs={{0,32},{32,64},{64,96},{96,0},{1,33},{33,65},{65,97},{97,1},{2,34}... | collective-permute-start | bytes 1572872 | tf_op jit(solution)/shard_map/ppermute | solution.py:386
  37.6 21.8 %collective-permute-start.8 = (f32[2,2,32,1024]{3,2,1,0:T(8,128)}, f32[2,2,32,1024]{3,2,1,0:T(8,128)S(1)}, u32[]{:S(2)}, u32[]{:S(2)}) collective-permute-start(f32[2,2,32,1024]{3,2,1,0:T(8,128)} %get-tuple-element.43), channel_id=1, source_target_pairs={{0,96},{32,0},{64,32},{96,64},{1,97},{33,1},{65,33},{97,65},{2,98}... | collective-permute-start | bytes 1572872 | tf_op jit(solution)/shard_map/ppermute | solution.py:386
  42.7 1.9 %collective-permute-start.3 = (f32[264,128]{1,0:T(8,128)S(1)}, f32[264,128]{1,0:T(8,128)S(1)}, u32[]{:S(2)}, u32[]{:S(2)}) collective-permute-start(f32[264,128]{1,0:T(8,128)S(1)} %get-tuple-element.37), channel_id=1, source_target_pairs={{0,1},{1,0},{2,3},{3,2},{4,5},{5,4},{6,7},{7,6},{8,9},{9,8},{10,11... | collective-permute-start | bytes 405512 | tf_op jit(solution)/shard_map/ppermute | solution.py:177
  44.7 4.2 %collective-permute-start.4 = (f32[264,128]{1,0:T(8,128)S(1)}, f32[264,128]{1,0:T(8,128)S(1)}, u32[]{:S(2)}, u32[]{:S(2)}) collective-permute-start(f32[264,128]{1,0:T(8,128)S(1)} %add.24), channel_id=1, source_target_pairs={{0,2},{1,9},{2,0},{3,11},{4,6},{5,13},{6,4},{7,15},{8,10},{9,1},{1... | collective-permute-start | bytes 405512 | tf_op jit(solution)/shard_map/ppermute | solution.py:177
  49.0 5.5 %collective-permute-start.5 = (f32[264,128]{1,0:T(8,128)S(1)}, f32[264,128]{1,0:T(8,128)S(1)}, u32[]{:S(2)}, u32[]{:S(2)}) collective-permute-start(f32[264,128]{1,0:T(8,128)S(1)} %add.25), channel_id=1, source_target_pairs={{0,6},{1,25},{2,4},{3,27},{4,2},{5,29},{6,0},{7,31},{8,14},{9,17},... | collective-permute-start | bytes 405512 | tf_op jit(solution)/shard_map/ppermute | solution.py:177
  61.1 2.3 %collective-permute-start.9 = (f32[264,128]{1,0:T(8,128)S(1)}, f32[264,128]{1,0:T(8,128)S(1)}, u32[]{:S(2)}, u32[]{:S(2)}) collective-permute-start(f32[264,128]{1,0:T(8,128)S(1)} %get-tuple-element.45), channel_id=1, source_target_pairs={{0,1},{1,0},{2,3},{3,2},{4,5},{5,4},{6,7},{7,6},{8,9},{9,8},{10,11... | collective-permute-start | bytes 405512 | tf_op jit(solution)/shard_map/ppermute | solution.py:177
  63.5 5.7 %collective-permute-start.10 = (f32[2,264,128]{2,1,0:T(8,128)S(1)}, f32[2,264,128]{2,1,0:T(8,128)S(1)}, u32[]{:S(2)}, u32[]{:S(2)}) collective-permute-start(f32[2,264,128]{2,1,0:T(8,128)S(1)} %pad_maximum_fusion), channel_id=1, source_target_pairs={{0,8},{1,3},{2,10},{3,1},{4,12},{5,7},{6,14},{7,5},{8,0},{9,11},{1... | collective-permute-start | bytes 811016 | tf_op jit(solution)/shard_map/ppermute | solution.py:177
  69.2 6.9 %collective-permute-start.11 = (f32[2,264,128]{2,1,0:T(8,128)S(1)}, f32[2,264,128]{2,1,0:T(8,128)S(1)}, u32[]{:S(2)}, u32[]{:S(2)}) collective-permute-start(f32[2,264,128]{2,1,0:T(8,128)S(1)} %fusion.1), channel_id=1, source_target_pairs={{0,24},{1,7},{2,26},{3,5},{4,28},{5,3},{6,30},{7,1},{8,16},{9,15},... | collective-permute-start | bytes 811016 | tf_op jit(solution)/shard_map/ppermute | solution.py:177
  76.2 4.7 %collective-permute-start.12 = (f32[264,128]{1,0:T(8,128)S(1)}, f32[264,128]{1,0:T(8,128)S(1)}, u32[]{:S(2)}, u32[]{:S(2)}) collective-permute-start(f32[264,128]{1,0:T(8,128)S(1)} %get-tuple-element.51), channel_id=1, source_target_pairs={{0,2},{1,9},{2,0},{3,11},{4,6},{5,13},{6,4},{7,15},{8,10},{9,1},{1... | collective-permute-start | bytes 405512 | tf_op jit(solution)/shard_map/ppermute | solution.py:177
  81.0 8.8 %collective-permute-start.13 = (f32[264,128]{1,0:T(8,128)S(1)}, f32[264,128]{1,0:T(8,128)S(1)}, u32[]{:S(2)}, u32[]{:S(2)}) collective-permute-start(f32[264,128]{1,0:T(8,128)S(1)} %fusion), channel_id=1, source_target_pairs={{0,6},{1,25},{2,4},{3,27},{4,2},{5,29},{6,0},{7,31},{8,14},{9,17},... | collective-permute-start | bytes 405512 | tf_op jit(solution)/shard_map/ppermute | solution.py:177
  86.4 10.5 %collective-permute-start.15 = (f32[2,256,256]{2,1,0:T(8,128)S(1)}, f32[2,256,256]{2,1,0:T(8,128)S(1)}, u32[]{:S(2)}, u32[]{:S(2)}) collective-permute-start(f32[2,256,256]{2,1,0:T(8,128)S(1)} %shard_map.55.mine_ref), channel_id=1, source_target_pairs={{0,1},{1,0},{2,3},{3,2},{4,5},{5,4},{6,7},{7,6},{8,9},{9,8},{10,11... | collective-permute-start | bytes 1572872 | tf_op jit(solution)/shard_map/ppermute | solution.py:177
  96.5 2.4 %collective-permute-start.14 = (f32[2,256,256]{2,1,0:T(8,128)S(1)}, f32[2,256,256]{2,1,0:T(8,128)S(1)}, u32[]{:S(2)}, u32[]{:S(2)}) collective-permute-start(f32[2,256,256]{2,1,0:T(8,128)S(1)} %shard_map.53.mine_ref), channel_id=1, source_target_pairs={{0,1},{1,0},{2,3},{3,2},{4,5},{5,4},{6,7},{7,6},{8,9},{9,8},{10,11... | collective-permute-start | bytes 1572872 | tf_op jit(solution)/shard_map/ppermute | solution.py:177

commit v4 on v3

--- a/solution.py
+++ b/solution.py
@@ -130,7 +130,11 @@
                 start = pl.multiple_of(c * n_all + source * n_seg, n_seg)
                 mt_ref[j, pl.ds(start, n_seg), :] = pieces[h][j, c]
         m = mt_ref[j]
-        g = dot3(m, m * vol_ref[...], ((1,), (1,)))
+        m = m * jnp.sqrt(vol_ref[...])
+        high = m.astype(jnp.bfloat16)
+        low = (m - high.astype(jnp.float32)).astype(jnp.bfloat16)
+        mixed = dot(high, low, ((1,), (1,)))
+        g = dot(high, high, ((1,), (1,))) + (mixed + mixed.T)
         g11, g21, g22 = g[:n_all, :n_all], g[n_all:, :n_all], g[n_all:, n_all:]
         packed[j, :n_all, :] = g21
         packed[j, n_all : 2 * n_all, :] = jnp.where(row >= col, g11, g22)

time: 101 us -> 101 us (level)
  no operation moved by 1% of the time
where the time goes in v4:
time: 101 us
  waiting for transfers between devices  40.6 us (40%)
  starting transfers between devices  30.6 us (30%)
  Pallas kernels  27.7 us (27%)
    ppermute x6, waiting for transfers between devices, on_device(): lax.ppermute(piece, 'freq', [(i, (i + hop) % n_freq) for i in range(n_fre...  24.3 us
    ppermute x10, starting transfers between devices, swap(): return lax.ppermute(value, 'space', space_pairs(kind))  17.3 us
    ppermute x10, waiting for transfers between devices, swap(): return lax.ppermute(value, 'space', space_pairs(kind))  16.3 us
    pallas_call x3, Pallas kernels, factor_call(): pl.pallas_call(functools.partial(factor_kernel, begin, end), out_shape=ja...  13.6 us
    ppermute x6, starting transfers between devices, on_device(): lax.ppermute(piece, 'freq', [(i, (i + hop) % n_freq) for i in range(n_fre...  13.3 us
    pallas_call x1, Pallas kernels, transform(): pl.pallas_call(transform_kernel, out_shape=shapes, in_specs=[IN_HBM, IN_H...  7.51 us
    pallas_call x2, Pallas kernels, modes_call(): pl.pallas_call(functools.partial(modes_kernel, js, root_rows), out_shape=...  4.15 us
    pallas_call x2, Pallas kernels, gram(): pl.pallas_call(gram_kernel, out_shape=[jax.ShapeDtypeStruct((nj, n, n_x),...  2.45 us
  transfers between devices with their start and end apart: 16, of which 9 were waited for; matrix products, arithmetic and copies ran while one was open for 0% of the time, Pallas kernels for 17%

profile of v4, /device:TPU:1, one launch (start us, length us, event | category | flops | bytes accessed | tf_op | source)
XLA Modules:
  0.0 100.8 jit_solution(7093161000324223458)
XLA Ops:
  0.6 0.0 copy-start.1
  0.6 0.6 copy-done.1
  1.3 0.0 copy-start
  1.3 7.5 %shard_map.50 = (f32[2,2,32,1024]{3,2,1,0:T(8,128)S(1)}, f32[2,2,32,1024]{3,2,1,0:T(8,128)S(1)}, f32[2,2,32,1024]{3,2,1,0:T(8,128)S(1)}, f32[2,2,32,1024]{3,2,1,...) custom-call(s32[16]{0:T(128)S(1)} %copy-done.1, ...), custom_call_target="tpu_custom_call" | custom-call | flops 1000 | bytes 1000 | tf_op jit(solution)/shard_map/pallas_call | solution.py:99
  8.8 4.5 %collective-permute-start = (f32[2,2,32,1024]{3,2,1,0:T(8,128)S(1)}, f32[2,2,32,1024]{3,2,1,0:T(8,128)S(1)}, u32[]{:S(2)}, u32[]{:S(2)}) collective-permute-start(f32[2,2,32,1024]{3,2,1,0:T(8,128)S(1)} %get-tuple-element.28), channel_id=1, source_target_pairs={{0,64},{32,96},{64,0},{96,32},{1,65},{33,97},{65,1},{97,33},{2,66}... | collective-permute-start | bytes 1572872 | tf_op jit(solution)/shard_map/ppermute | solution.py:390
  13.3 0.7 collective-permute-start.1
  14.1 1.9 %collective-permute-start.2 = (f32[2,2,32,1024]{3,2,1,0:T(8,128)S(1)}, f32[2,2,32,1024]{3,2,1,0:T(8,128)S(1)}, u32[]{:S(2)}, u32[]{:S(2)}) collective-permute-start(f32[2,2,32,1024]{3,2,1,0:T(8,128)S(1)} %get-tuple-element.34), channel_id=1, source_target_pairs={{0,96},{32,0},{64,32},{96,64},{1,97},{33,1},{65,33},{97,65},{2,98}... | collective-permute-start | bytes 1572872 | tf_op jit(solution)/shard_map/ppermute | solution.py:390
  16.0 9.0 %collective-permute-done.refs_1_ = f32[2,2,32,1024]{3,2,1,0:T(8,128)S(1)} collective-permute-done((f32[2,2,32,1024]{3,2,1,0:T(8,128)S(1)}, f32[2,2,32,1024]{3,2,1,0:T(8,128)S(1)}, u32[]{:S(2)}, u32[]{:S(2)}) %collective-permute-start) | collective-permute-done | bytes 524320 | tf_op jit(solution)/shard_map/ppermute | solution.py:390
  25.0 2.7 %collective-permute-start.6 = (f32[2,2,32,1024]{3,2,1,0:T(8,128)S(1)}, f32[2,2,32,1024]{3,2,1,0:T(8,128)S(1)}, u32[]{:S(2)}, u32[]{:S(2)}) collective-permute-start(f32[2,2,32,1024]{3,2,1,0:T(8,128)S(1)} %get-tuple-element.41), channel_id=1, source_target_pairs={{0,64},{32,96},{64,0},{96,32},{1,65},{33,97},{65,1},{97,33},{2,66}... | collective-permute-start | bytes 1572872 | tf_op jit(solution)/shard_map/ppermute | solution.py:390
  27.7 9.9 %collective-permute-done.1.refs_2_ = f32[2,2,32,1024]{3,2,1,0:T(8,128)S(1)} collective-permute-done((f32[2,2,32,1024]{3,2,1,0:T(8,128)S(1)}, f32[2,2,32,1024]{3,2,1,0:T(8,128)S(1)}, u32[]{:S(2)}, u32[]{:S(2)}) %collective-permute-start.1) | collective-permute-done | bytes 524320 | tf_op jit(solution)/shard_map/ppermute | solution.py:390
  37.6 0.0 collective-permute-start.7
  37.6 0.0 collective-permute-done.2.refs_3_
  37.6 3.4 %collective-permute-start.8 = (f32[2,2,32,1024]{3,2,1,0:T(8,128)}, f32[2,2,32,1024]{3,2,1,0:T(8,128)S(1)}, u32[]{:S(2)}, u32[]{:S(2)}) collective-permute-start(f32[2,2,32,1024]{3,2,1,0:T(8,128)} %get-tuple-element.43), channel_id=1, source_target_pairs={{0,96},{32,0},{64,32},{96,64},{1,97},{33,1},{65,33},{97,65},{2,98}... | collective-permute-start | bytes 1572872 | tf_op jit(solution)/shard_map/ppermute | solution.py:390
  41.1 0.0 copy-done
  41.1 1.2 %shard_map.51 = (f32[2,256,1024]{2,1,0:T(8,128)S(1)}, f32[264,128]{1,0:T(8,128)S(1)}, f32[264,128]{1,0:T(8,128)S(1)}) custom-call(f32[1,1024]{1,0:T(1,128)S(1)} %bitcast.11, f32[2,2,32,1024]{3,2,1,0:T(8,128)S(1)} %get-tuple-element.26.refs_0_, f32[2,2,32,1024]{3,2,1,0:T(8,128)S(1)} %collective-permute-done.refs_1_, ...), custom_call_target="tpu_custom_call" | custom-call | flops 1000 | bytes 1000 | tf_op jit(solution)/shard_map/pallas_call | solution.py:151
  42.3 0.9 collective-permute-start.3
  43.3 1.0 collective-permute-done.3
  44.3 1.4 %collective-permute-start.4 = (f32[264,128]{1,0:T(8,128)S(1)}, f32[264,128]{1,0:T(8,128)S(1)}, u32[]{:S(2)}, u32[]{:S(2)}) collective-permute-start(f32[264,128]{1,0:T(8,128)S(1)} %add.24), channel_id=1, source_target_pairs={{0,2},{1,9},{2,0},{3,11},{4,6},{5,13},{6,4},{7,15},{8,10},{9,1},{1... | collective-permute-start | bytes 405512 | tf_op jit(solution)/shard_map/ppermute | solution.py:181
  45.6 2.9 %collective-permute-done.4 = f32[264,128]{1,0:T(8,128)S(1)} collective-permute-done((f32[264,128]{1,0:T(8,128)S(1)}, f32[264,128]{1,0:T(8,128)S(1)}, u32[]{:S(2)}, u32[]{:S(2)}) %collective-permute-start.4) | collective-permute-done | bytes 135200 | tf_op jit(solution)/shard_map/ppermute | solution.py:181
  48.5 2.8 %collective-permute-start.5 = (f32[264,128]{1,0:T(8,128)S(1)}, f32[264,128]{1,0:T(8,128)S(1)}, u32[]{:S(2)}, u32[]{:S(2)}) collective-permute-start(f32[264,128]{1,0:T(8,128)S(1)} %add.25), channel_id=1, source_target_pairs={{0,6},{1,25},{2,4},{3,27},{4,2},{5,29},{6,0},{7,31},{8,14},{9,17},... | collective-permute-start | bytes 405512 | tf_op jit(solution)/shard_map/ppermute | solution.py:181
  51.3 2.7 %collective-permute-done.5 = f32[264,128]{1,0:T(8,128)S(1)} collective-permute-done((f32[264,128]{1,0:T(8,128)S(1)}, f32[264,128]{1,0:T(8,128)S(1)}, u32[]{:S(2)}, u32[]{:S(2)}) %collective-permute-start.5) | collective-permute-done | bytes 135200 | tf_op jit(solution)/shard_map/ppermute | solution.py:181
  54.0 0.0 collective-permute-done.6.refs_1_
  54.1 5.4 %collective-permute-done.7.refs_2_ = f32[2,2,32,1024]{3,2,1,0:T(8,128)S(1)} collective-permute-done((f32[2,2,32,1024]{3,2,1,0:T(8,128)S(1)}, f32[2,2,32,1024]{3,2,1,0:T(8,128)S(1)}, u32[]{:S(2)}, u32[]{:S(2)}) %collective-permute-start.7) | collective-permute-done | bytes 524320 | tf_op jit(solution)/shard_map/ppermute | solution.py:390
  59.4 0.0 collective-permute-done.8.refs_3_
  59.5 1.2 %shard_map.52 = (f32[2,256,1024]{2,1,0:T(8,128)S(1)}, f32[264,128]{1,0:T(8,128)S(1)}, f32[264,128]{1,0:T(8,128)S(1)}) custom-call(f32[1,1024]{1,0:T(1,128)S(1)} %bitcast.12, f32[2,2,32,1024]{3,2,1,0:T(8,128)S(1)} %get-tuple-element.40.refs_0_, f32[2,2,32,1024]{3,2,1,0:T(8,128)S(1)} %collective-permute-done.6.refs_1_, ...), custom_call_target="tpu_custom_call" | custom-call | flops 1000 | bytes 1000 | tf_op jit(solution)/shard_map/pallas_call | solution.py:151
  60.7 1.3 %collective-permute-start.9 = (f32[264,128]{1,0:T(8,128)S(1)}, f32[264,128]{1,0:T(8,128)S(1)}, u32[]{:S(2)}, u32[]{:S(2)}) collective-permute-start(f32[264,128]{1,0:T(8,128)S(1)} %get-tuple-element.45), channel_id=1, source_target_pairs={{0,1},{1,0},{2,3},{3,2},{4,5},{5,4},{6,7},{7,6},{8,9},{9,8},{10,11... | collective-permute-start | bytes 405512 | tf_op jit(solution)/shard_map/ppermute | solution.py:181
  62.0 1.0 collective-permute-done.9
  63.1 1.3 %collective-permute-start.10 = (f32[2,264,128]{2,1,0:T(8,128)S(1)}, f32[2,264,128]{2,1,0:T(8,128)S(1)}, u32[]{:S(2)}, u32[]{:S(2)}) collective-permute-start(f32[2,264,128]{2,1,0:T(8,128)S(1)} %pad_maximum_fusion), channel_id=1, source_target_pairs={{0,8},{1,3},{2,10},{3,1},{4,12},{5,7},{6,14},{7,5},{8,0},{9,11},{1... | collective-permute-start | bytes 811016 | tf_op jit(solution)/shard_map/ppermute | solution.py:181
  64.4 4.4 %collective-permute-done.10 = f32[2,264,128]{2,1,0:T(8,128)S(1)} collective-permute-done((f32[2,264,128]{2,1,0:T(8,128)S(1)}, f32[2,264,128]{2,1,0:T(8,128)S(1)}, u32[]{:S(2)}, u32[]{:S(2)}) %collective-permute-start.10) | collective-permute-done | bytes 270368 | tf_op jit(solution)/shard_map/ppermute | solution.py:181
  68.7 0.1 fusion.1
  68.8 2.6 %collective-permute-start.11 = (f32[2,264,128]{2,1,0:T(8,128)S(1)}, f32[2,264,128]{2,1,0:T(8,128)S(1)}, u32[]{:S(2)}, u32[]{:S(2)}) collective-permute-start(f32[2,264,128]{2,1,0:T(8,128)S(1)} %fusion.1), channel_id=1, source_target_pairs={{0,24},{1,7},{2,26},{3,5},{4,28},{5,3},{6,30},{7,1},{8,16},{9,15},... | collective-permute-start | bytes 811016 | tf_op jit(solution)/shard_map/ppermute | solution.py:181
  71.4 4.3 %collective-permute-done.11 = f32[2,264,128]{2,1,0:T(8,128)S(1)} collective-permute-done((f32[2,264,128]{2,1,0:T(8,128)S(1)}, f32[2,264,128]{2,1,0:T(8,128)S(1)}, u32[]{:S(2)}, u32[]{:S(2)}) %collective-permute-start.11) | collective-permute-done | bytes 270368 | tf_op jit(solution)/shard_map/ppermute | solution.py:181
  75.7 0.1 fusion.2
  75.8 1.1 %collective-permute-start.12 = (f32[264,128]{1,0:T(8,128)S(1)}, f32[264,128]{1,0:T(8,128)S(1)}, u32[]{:S(2)}, u32[]{:S(2)}) collective-permute-start(f32[264,128]{1,0:T(8,128)S(1)} %get-tuple-element.51), channel_id=1, source_target_pairs={{0,2},{1,9},{2,0},{3,11},{4,6},{5,13},{6,4},{7,15},{8,10},{9,1},{1... | collective-permute-start | bytes 405512 | tf_op jit(solution)/shard_map/ppermute | solution.py:181
  76.9 3.6 %shard_map.54.in_ref = f32[256,512]{1,0:T(8,128)S(1)} custom-call(f32[264,128]{1,0:T(8,128)S(1)} %get-tuple-element.50.in_ref), custom_call_target="tpu_custom_call" | custom-call | flops 2147483648 | bytes 1000 | tf_op jit(solution)/shard_map/pallas_call | solution.py:301
  80.5 0.0 collective-permute-done.12
  80.5 2.2 %collective-permute-start.13 = (f32[264,128]{1,0:T(8,128)S(1)}, f32[264,128]{1,0:T(8,128)S(1)}, u32[]{:S(2)}, u32[]{:S(2)}) collective-permute-start(f32[264,128]{1,0:T(8,128)S(1)} %fusion), channel_id=1, source_target_pairs={{0,6},{1,25},{2,4},{3,27},{4,2},{5,29},{6,0},{7,31},{8,14},{9,17},... | collective-permute-start | bytes 405512 | tf_op jit(solution)/shard_map/ppermute | solution.py:181
  82.7 3.2 %shard_map.55.mine_ref = f32[2,256,256]{2,1,0:T(8,128)S(1)} custom-call(f32[256,512]{1,0:T(8,128)S(1)} %shard_map.54.in_ref), custom_call_target="tpu_custom_call" | custom-call | flops 2147483648 | bytes 1000 | tf_op jit(solution)/shard_map/pallas_call | solution.py:301
  86.0 3.3 %collective-permute-start.15 = (f32[2,256,256]{2,1,0:T(8,128)S(1)}, f32[2,256,256]{2,1,0:T(8,128)S(1)}, u32[]{:S(2)}, u32[]{:S(2)}) collective-permute-start(f32[2,256,256]{2,1,0:T(8,128)S(1)} %shard_map.55.mine_ref), channel_id=1, source_target_pairs={{0,1},{1,0},{2,3},{3,2},{4,5},{5,4},{6,7},{7,6},{8,9},{9,8},{10,11... | collective-permute-start | bytes 1572872 | tf_op jit(solution)/shard_map/ppermute | solution.py:181
  89.3 0.0 collective-permute-done.13
  89.3 6.8 %shard_map.53.mine_ref = f32[2,256,256]{2,1,0:T(8,128)S(1)} custom-call(f32[264,128]{1,0:T(8,128)S(1)} %add.31.in_ref), custom_call_target="tpu_custom_call" | custom-call | flops 4294967296 | bytes 1000 | tf_op jit(solution)/shard_map/pallas_call | solution.py:301
  96.1 0.3 collective-permute-start.14
  96.4 0.0 collective-permute-done.15.other_ref
  96.4 2.1 %shard_map.56 = (f32[4,1024,256]{2,1,0:T(8,128)}, f32[4,256,256]{2,1,0:T(8,128)}) custom-call(f32[2,256,256]{2,1,0:T(8,128)S(1)} %shard_map.55.mine_ref, f32[2,256,256]{2,1,0:T(8,128)S(1)} %collective-permute-done.15.other_ref, f32[2,256,1024]{2,1,0:T(8,128)S(1)} %get-tuple-element.47.mt_ref), custom_call_target="tpu_custom_call" | custom-call | flops 1000 | bytes 1000 | tf_op jit(solution)/shard_map/pallas_call | solution.py:355
  98.5 0.0 collective-permute-done.14.other_ref
  98.5 2.1 %shard_map.57 = (f32[4,1024,256]{2,1,0:T(8,128)}, f32[4,256,256]{2,1,0:T(8,128)}) custom-call(f32[2,256,256]{2,1,0:T(8,128)S(1)} %shard_map.53.mine_ref, f32[2,256,256]{2,1,0:T(8,128)S(1)} %collective-permute-done.14.other_ref, f32[2,256,1024]{2,1,0:T(8,128)S(1)} %get-tuple-element.46.mt_ref, ...), custom_call_target="tpu_custom_call", output_to_operand_aliasing={{0}: (3, {}), {1}: (4, {})} | custom-call | flops 1000 | bytes 1000 | tf_op jit(solution)/shard_map/pallas_call | solution.py:355
  (8 shorter events, 0.2 us)
Async XLA Ops:
  0.6 0.7 copy-start.1
  1.3 39.8 %copy-start = (f32[1024]{0:T(1024)S(1)}, f32[1024]{0:T(1024)}, u32[]{:S(2)}) copy-start(f32[1024]{0:T(1024)} %param.4) | copy-start | bytes 12292
  8.8 16.2 %collective-permute-start = (f32[2,2,32,1024]{3,2,1,0:T(8,128)S(1)}, f32[2,2,32,1024]{3,2,1,0:T(8,128)S(1)}, u32[]{:S(2)}, u32[]{:S(2)}) collective-permute-start(f32[2,2,32,1024]{3,2,1,0:T(8,128)S(1)} %get-tuple-element.28), channel_id=1, source_target_pairs={{0,64},{32,96},{64,0},{96,32},{1,65},{33,97},{65,1},{97,33},{2,66}... | collective-permute-start | bytes 1572872 | tf_op jit(solution)/shard_map/ppermute | solution.py:390
  13.3 24.3 %collective-permute-start.1 = (f32[2,2,32,1024]{3,2,1,0:T(8,128)S(1)}, f32[2,2,32,1024]{3,2,1,0:T(8,128)S(1)}, u32[]{:S(2)}, u32[]{:S(2)}) collective-permute-start(f32[2,2,32,1024]{3,2,1,0:T(8,128)S(1)} %get-tuple-element.31), channel_id=1, source_target_pairs={{0,32},{32,64},{64,96},{96,0},{1,33},{33,65},{65,97},{97,1},{2,34}... | collective-permute-start | bytes 1572872 | tf_op jit(solution)/shard_map/ppermute | solution.py:390
  14.1 23.6 %collective-permute-start.2 = (f32[2,2,32,1024]{3,2,1,0:T(8,128)S(1)}, f32[2,2,32,1024]{3,2,1,0:T(8,128)S(1)}, u32[]{:S(2)}, u32[]{:S(2)}) collective-permute-start(f32[2,2,32,1024]{3,2,1,0:T(8,128)S(1)} %get-tuple-element.34), channel_id=1, source_target_pairs={{0,96},{32,0},{64,32},{96,64},{1,97},{33,1},{65,33},{97,65},{2,98}... | collective-permute-start | bytes 1572872 | tf_op jit(solution)/shard_map/ppermute | solution.py:390
  25.0 29.0 %collective-permute-start.6 = (f32[2,2,32,1024]{3,2,1,0:T(8,128)S(1)}, f32[2,2,32,1024]{3,2,1,0:T(8,128)S(1)}, u32[]{:S(2)}, u32[]{:S(2)}) collective-permute-start(f32[2,2,32,1024]{3,2,1,0:T(8,128)S(1)} %get-tuple-element.41), channel_id=1, source_target_pairs={{0,64},{32,96},{64,0},{96,32},{1,65},{33,97},{65,1},{97,33},{2,66}... | collective-permute-start | bytes 1572872 | tf_op jit(solution)/shard_map/ppermute | solution.py:390
  37.6 21.8 %collective-permute-start.7 = (f32[2,2,32,1024]{3,2,1,0:T(8,128)S(1)}, f32[2,2,32,1024]{3,2,1,0:T(8,128)S(1)}, u32[]{:S(2)}, u32[]{:S(2)}) collective-permute-start(f32[2,2,32,1024]{3,2,1,0:T(8,128)S(1)} %get-tuple-element.42), channel_id=1, source_target_pairs={{0,32},{32,64},{64,96},{96,0},{1,33},{33,65},{65,97},{97,1},{2,34}... | collective-permute-start | bytes 1572872 | tf_op jit(solution)/shard_map/ppermute | solution.py:390
  37.6 21.8 %collective-permute-start.8 = (f32[2,2,32,1024]{3,2,1,0:T(8,128)}, f32[2,2,32,1024]{3,2,1,0:T(8,128)S(1)}, u32[]{:S(2)}, u32[]{:S(2)}) collective-permute-start(f32[2,2,32,1024]{3,2,1,0:T(8,128)} %get-tuple-element.43), channel_id=1, source_target_pairs={{0,96},{32,0},{64,32},{96,64},{1,97},{33,1},{65,33},{97,65},{2,98}... | collective-permute-start | bytes 1572872 | tf_op jit(solution)/shard_map/ppermute | solution.py:390
  42.3 1.9 %collective-permute-start.3 = (f32[264,128]{1,0:T(8,128)S(1)}, f32[264,128]{1,0:T(8,128)S(1)}, u32[]{:S(2)}, u32[]{:S(2)}) collective-permute-start(f32[264,128]{1,0:T(8,128)S(1)} %get-tuple-element.37), channel_id=1, source_target_pairs={{0,1},{1,0},{2,3},{3,2},{4,5},{5,4},{6,7},{7,6},{8,9},{9,8},{10,11... | collective-permute-start | bytes 405512 | tf_op jit(solution)/shard_map/ppermute | solution.py:181
  44.3 4.2 %collective-permute-start.4 = (f32[264,128]{1,0:T(8,128)S(1)}, f32[264,128]{1,0:T(8,128)S(1)}, u32[]{:S(2)}, u32[]{:S(2)}) collective-permute-start(f32[264,128]{1,0:T(8,128)S(1)} %add.24), channel_id=1, source_target_pairs={{0,2},{1,9},{2,0},{3,11},{4,6},{5,13},{6,4},{7,15},{8,10},{9,1},{1... | collective-permute-start | bytes 405512 | tf_op jit(solution)/shard_map/ppermute | solution.py:181
  48.5 5.5 %collective-permute-start.5 = (f32[264,128]{1,0:T(8,128)S(1)}, f32[264,128]{1,0:T(8,128)S(1)}, u32[]{:S(2)}, u32[]{:S(2)}) collective-permute-start(f32[264,128]{1,0:T(8,128)S(1)} %add.25), channel_id=1, source_target_pairs={{0,6},{1,25},{2,4},{3,27},{4,2},{5,29},{6,0},{7,31},{8,14},{9,17},... | collective-permute-start | bytes 405512 | tf_op jit(solution)/shard_map/ppermute | solution.py:181
  60.7 2.3 %collective-permute-start.9 = (f32[264,128]{1,0:T(8,128)S(1)}, f32[264,128]{1,0:T(8,128)S(1)}, u32[]{:S(2)}, u32[]{:S(2)}) collective-permute-start(f32[264,128]{1,0:T(8,128)S(1)} %get-tuple-element.45), channel_id=1, source_target_pairs={{0,1},{1,0},{2,3},{3,2},{4,5},{5,4},{6,7},{7,6},{8,9},{9,8},{10,11... | collective-permute-start | bytes 405512 | tf_op jit(solution)/shard_map/ppermute | solution.py:181
  63.1 5.7 %collective-permute-start.10 = (f32[2,264,128]{2,1,0:T(8,128)S(1)}, f32[2,264,128]{2,1,0:T(8,128)S(1)}, u32[]{:S(2)}, u32[]{:S(2)}) collective-permute-start(f32[2,264,128]{2,1,0:T(8,128)S(1)} %pad_maximum_fusion), channel_id=1, source_target_pairs={{0,8},{1,3},{2,10},{3,1},{4,12},{5,7},{6,14},{7,5},{8,0},{9,11},{1... | collective-permute-start | bytes 811016 | tf_op jit(solution)/shard_map/ppermute | solution.py:181
  68.8 6.9 %collective-permute-start.11 = (f32[2,264,128]{2,1,0:T(8,128)S(1)}, f32[2,264,128]{2,1,0:T(8,128)S(1)}, u32[]{:S(2)}, u32[]{:S(2)}) collective-permute-start(f32[2,264,128]{2,1,0:T(8,128)S(1)} %fusion.1), channel_id=1, source_target_pairs={{0,24},{1,7},{2,26},{3,5},{4,28},{5,3},{6,30},{7,1},{8,16},{9,15},... | collective-permute-start | bytes 811016 | tf_op jit(solution)/shard_map/ppermute | solution.py:181
  75.8 4.7 %collective-permute-start.12 = (f32[264,128]{1,0:T(8,128)S(1)}, f32[264,128]{1,0:T(8,128)S(1)}, u32[]{:S(2)}, u32[]{:S(2)}) collective-permute-start(f32[264,128]{1,0:T(8,128)S(1)} %get-tuple-element.51), channel_id=1, source_target_pairs={{0,2},{1,9},{2,0},{3,11},{4,6},{5,13},{6,4},{7,15},{8,10},{9,1},{1... | collective-permute-start | bytes 405512 | tf_op jit(solution)/shard_map/ppermute | solution.py:181
  80.5 8.8 %collective-permute-start.13 = (f32[264,128]{1,0:T(8,128)S(1)}, f32[264,128]{1,0:T(8,128)S(1)}, u32[]{:S(2)}, u32[]{:S(2)}) collective-permute-start(f32[264,128]{1,0:T(8,128)S(1)} %fusion), channel_id=1, source_target_pairs={{0,6},{1,25},{2,4},{3,27},{4,2},{5,29},{6,0},{7,31},{8,14},{9,17},... | collective-permute-start | bytes 405512 | tf_op jit(solution)/shard_map/ppermute | solution.py:181
  86.0 10.5 %collective-permute-start.15 = (f32[2,256,256]{2,1,0:T(8,128)S(1)}, f32[2,256,256]{2,1,0:T(8,128)S(1)}, u32[]{:S(2)}, u32[]{:S(2)}) collective-permute-start(f32[2,256,256]{2,1,0:T(8,128)S(1)} %shard_map.55.mine_ref), channel_id=1, source_target_pairs={{0,1},{1,0},{2,3},{3,2},{4,5},{5,4},{6,7},{7,6},{8,9},{9,8},{10,11... | collective-permute-start | bytes 1572872 | tf_op jit(solution)/shard_map/ppermute | solution.py:181
  96.1 2.4 %collective-permute-start.14 = (f32[2,256,256]{2,1,0:T(8,128)S(1)}, f32[2,256,256]{2,1,0:T(8,128)S(1)}, u32[]{:S(2)}, u32[]{:S(2)}) collective-permute-start(f32[2,256,256]{2,1,0:T(8,128)S(1)} %shard_map.53.mine_ref), channel_id=1, source_target_pairs={{0,1},{1,0},{2,3},{3,2},{4,5},{5,4},{6,7},{7,6},{8,9},{9,8},{10,11... | collective-permute-start | bytes 1572872 | tf_op jit(solution)/shard_map/ppermute | solution.py:181
